TPU v7x, 32 devices: a whole 2x2x4 slice. The times are simulated.
32 devices in a mesh: items: 4 (over y, x), seq: 8 (over z, core).
Axes of the slice: x: 2, y: 2, z: 4, core: 2. Of those that a mesh axis runs over, the one named last changes fastest.
Arguments:
- features: float32 [4, 4096, 1024], P('items', 'seq'), may hold values from -6 to 6
- item_spans: int32 [4, 8], P('items'), may hold values from 0 to 3, as said below
- item_lengths: int32 [4, 8], P('items'), may hold values from 0 to 1500, as said below
- ffn1_gain: bfloat16 [1024], P(('items', 'seq')), may hold values from 0.25 to 1.75
- ffn1_in: bfloat16 [1024, 4096], P(('items', 'seq')), may hold values from -0.1875 to 0.1875
- ffn1_out: bfloat16 [4096, 1024], P(('items', 'seq')), may hold values from -0.09375 to 0.09375
- att_gain: bfloat16 [1024], P(('items', 'seq')), may hold values from 0.25 to 1.75
- w_query: bfloat16 [1024, 1024], P(('items', 'seq')), may hold values from -0.1875 to 0.1875
- w_key: bfloat16 [1024, 1024], P(('items', 'seq')), may hold values from -0.1875 to 0.1875
- w_value: bfloat16 [1024, 1024], P(('items', 'seq')), may hold values from -0.1875 to 0.1875
- w_pos: bfloat16 [1024, 1024], P(('items', 'seq')), may hold values from -0.1875 to 0.1875
- u_bias: bfloat16 [1024], P(('items', 'seq')), may hold values from -3 to 3
- v_bias: bfloat16 [1024], P(('items', 'seq')), may hold values from -3 to 3
- w_out: bfloat16 [1024, 1024], P(('items', 'seq')), may hold values from -1.5 to 1.5
- conv_gain: bfloat16 [1024], P(('items', 'seq')), may hold values from 0.25 to 1.75
- conv_in: bfloat16 [1024, 2048], P(('items', 'seq')), may hold values from -0.1875 to 0.1875
- depth_kernel: bfloat16 [31, 1024], P(None, ('items', 'seq')), may hold values from -1 to 1
- inner_gain: bfloat16 [1024], P(('items', 'seq')), may hold values from 0.25 to 1.75
- conv_out: bfloat16 [1024, 1024], P(('items', 'seq')), may hold values from -0.1875 to 0.1875
- ffn2_gain: bfloat16 [1024], P(('items', 'seq')), may hold values from 0.25 to 1.75
- ffn2_in: bfloat16 [1024, 4096], P(('items', 'seq')), may hold values from -0.1875 to 0.1875
- ffn2_out: bfloat16 [4096, 1024], P(('items', 'seq')), may hold values from -0.09375 to 0.09375
- final_gain: bfloat16 [1024], P(('items', 'seq')), may hold values from 0.25 to 1.75
- cotangent: float32 [4, 4096, 1024], P('items', 'seq'), may hold values from -6 to 6
Outputs:
- layer_out: float32 [4, 4096, 1024], P('items', 'seq')
- input_grad: float32 [4, 4096, 1024], P('items', 'seq')
- grad_ffn1_gain: float32 [1024], P(('items', 'seq'))
- grad_ffn1_in: float32 [1024, 4096], P(('items', 'seq'))
- grad_ffn1_out: float32 [4096, 1024], P(('items', 'seq'))
- grad_att_gain: float32 [1024], P(('items', 'seq'))
- grad_w_query: float32 [1024, 1024], P(('items', 'seq'))
- grad_w_key: float32 [1024, 1024], P(('items', 'seq'))
- grad_w_value: float32 [1024, 1024], P(('items', 'seq'))
- grad_w_pos: float32 [1024, 1024], P(('items', 'seq'))
- grad_u_bias: float32 [1024], P(('items', 'seq'))
- grad_v_bias: float32 [1024], P(('items', 'seq'))
- grad_w_out: float32 [1024, 1024], P(('items', 'seq'))
- grad_conv_gain: float32 [1024], P(('items', 'seq'))
- grad_conv_in: float32 [1024, 2048], P(('items', 'seq'))
- grad_depth_kernel: float32 [31, 1024], P(None, ('items', 'seq'))
- grad_inner_gain: float32 [1024], P(('items', 'seq'))
- grad_conv_out: float32 [1024, 1024], P(('items', 'seq'))
- grad_ffn2_gain: float32 [1024], P(('items', 'seq'))
- grad_ffn2_in: float32 [1024, 4096], P(('items', 'seq'))
- grad_ffn2_out: float32 [4096, 1024], P(('items', 'seq'))
- grad_final_gain: float32 [1024], P(('items', 'seq'))
Inputs may be any that keep to these rules, and one draw needn't show every extreme that they name: `item_spans`: in each group every block either starts an item, holding its number of blocks (3 or 2 for a long item, 1 for a short one in this block alone), or holds 0 and continues the item started before it. Block 0 starts a long item, a long item of 3 blocks starts at block 3 or 2, and the last block ends a long item. `item_lengths`: valid frames of the item that starts in a block: 1025 to 1500 for an item of 3 blocks, 768 to 1024 for one of 2 blocks, 125 to 500 for a short one, 0 in blocks that continue an item. The item of 3 blocks near the middle has exactly 1500.
All inputs are finite; a program needn't handle non-finite values.
Results may differ from a plain program's by a relative error of at most 0.018.
Values may be sent and summed in bfloat16 or wider, within the bound.
A program may use at most 384 MiB of HBM per device.

v0:
```python
import jax
import jax.numpy as jnp
from jax import lax
from jax.sharding import PartitionSpec as P

HEAD_DIM = 64
TAPS = 31
BLOCK = 512


EPSILON = 1e-05


def padded(array, sides, width):
    for axis, dim in sides:
        size, length = (lax.axis_size(axis), array.shape[dim])
        up = [(i, (i + 1) % size) for i in range(size - 1)]
        down = [(j, i) for i, j in up]
        last = lax.slice_in_dim(array, length - width, length, axis=dim)
        initial = lax.slice_in_dim(array, 0, width, axis=dim)
        before = lax.ppermute(last, axis, up)
        after = lax.ppermute(initial, axis, down)
        array = jnp.concatenate([before, array, after], axis=dim)
    return array


def plain_round(v):
    return lax.optimization_barrier(v.astype(jnp.bfloat16)).astype(jnp.float32)


def make_value_round():
    wrapped = jax.custom_vjp(plain_round)

    def value_keep(v):
        return (plain_round(v), None)

    def value_pass(kept, grad):
        return (grad,)

    wrapped.defvjp(value_keep, value_pass)
    return wrapped


def make_grad_round():

    def identity_value(v):
        return v

    wrapped = jax.custom_vjp(identity_value)

    def grad_keep(v):
        return (v, None)

    def grad_pass(kept, grad):
        return (plain_round(grad),)

    wrapped.defvjp(grad_keep, grad_pass)
    return wrapped


def make_low_product():

    def low_dot(left_side, right_side):
        return jnp.dot(
            left_side.astype(jnp.bfloat16),
            right_side.astype(jnp.bfloat16),
            preferred_element_type=jnp.float32,
        )

    wrapped = jax.custom_vjp(low_dot)

    def product_keep(left_side, right_side):
        left_low = left_side.astype(jnp.bfloat16)
        right_low = right_side.astype(jnp.bfloat16)
        return (
            jnp.dot(left_low, right_low, preferred_element_type=jnp.float32),
            (left_low, right_low),
        )

    def product_back(kept, grad):
        left_low, right_low = kept
        grad_low = grad.astype(jnp.bfloat16)
        left_grad = jnp.dot(grad_low, right_low.T, preferred_element_type=jnp.float32)
        right_grad = jnp.dot(left_low.T, grad_low, preferred_element_type=jnp.float32)
        return (left_grad, right_grad)

    wrapped.defvjp(product_keep, product_back)
    return wrapped


def round_value(v):
    return make_value_round()(v)


def round_grad(v):
    return make_grad_round()(v)


def product(left_side, right_side):
    return make_low_product()(left_side, right_side)


def layer_norm(values, norm_gain):
    center = values - jnp.mean(values, axis=-1, keepdims=True)
    spread = jnp.mean(center * center, axis=-1, keepdims=True)
    return center * lax.rsqrt(spread + EPSILON) * norm_gain


def block_layout(span_row, length_row):
    places = jnp.arange(span_row.shape[0], dtype=jnp.int32)
    item_start = lax.cummax(jnp.where(span_row > 0, places, 0), axis=0)
    item_length = jnp.take(length_row, item_start)
    return (item_start, item_length)


def frame_items(frame_index, item_start, item_length, extent):
    inside = (frame_index >= 0) & (frame_index < extent)
    block_index = jnp.clip(frame_index // BLOCK, 0, item_start.shape[0] - 1)
    owner_item = jnp.take(item_start, block_index)
    valid_frame = inside & (frame_index - owner_item * BLOCK < jnp.take(item_length, block_index))
    return (jnp.where(inside, owner_item, -1), valid_frame)


def same_item(owners_wide, extent):
    half_taps = (TAPS - 1) // 2
    center = owners_wide[half_taps : half_taps + extent]
    columns = [owners_wide[tap_index : tap_index + extent] == center for tap_index in range(TAPS)]
    return jnp.stack(columns, axis=1).astype(jnp.float32)


def relative_table(model_width):
    distance = (3 * BLOCK - 1 - jnp.arange(6 * BLOCK)).astype(jnp.float32)
    frequency = 1.0 / 10000.0 ** (jnp.arange(0, model_width, 2).astype(jnp.float32) / model_width)
    angles = distance[:, None] * frequency[None, :]
    return jnp.concatenate([jnp.sin(angles), jnp.cos(angles)], axis=1)


def relative_shift(positional):
    flattened = positional.reshape(-1)
    diagonal_band = lax.slice(flattened, (BLOCK - 1,), (BLOCK - 1 + BLOCK * (2 * BLOCK - 1),))
    return diagonal_band.reshape(BLOCK, 2 * BLOCK - 1)[:, :BLOCK]


def attend_head(
    queries, keys_h, values_h, content_bias, position_bias, relative, item_start, item_length
):
    frames = queries.shape[0]
    block_count = frames // BLOCK
    factor = HEAD_DIM ** (-0.5)
    key_bias = jnp.sum(keys_h * content_bias, axis=1)
    rel_bias = jnp.sum(relative * position_bias, axis=1)
    offsets = jnp.arange(BLOCK, dtype=jnp.int32)

    def one_block(block_index):
        query_rows = lax.dynamic_slice_in_dim(queries, block_index * BLOCK, BLOCK, 0)
        first_block = jnp.take(item_start, block_index)
        item_frames = jnp.take(item_length, block_index)
        score_parts = []
        value_parts = []
        for step_index in range(3):
            key_block = jnp.minimum(first_block + step_index, block_count - 1)
            key_rows = lax.dynamic_slice_in_dim(keys_h, key_block * BLOCK, BLOCK, 0)
            value_rows = lax.dynamic_slice_in_dim(values_h, key_block * BLOCK, BLOCK, 0)
            bias_rows = lax.dynamic_slice_in_dim(key_bias, key_block * BLOCK, BLOCK, 0)
            content = product(query_rows, key_rows.T) + bias_rows[None, :]
            distance_base = jnp.clip((block_index - key_block) * BLOCK, -2 * BLOCK, 2 * BLOCK)
            window = lax.dynamic_slice_in_dim(relative, 2 * BLOCK - distance_base, 2 * BLOCK, 0)
            window_bias = lax.dynamic_slice_in_dim(
                rel_bias, 2 * BLOCK - distance_base, 2 * BLOCK, 0
            )
            positional = product(query_rows, window.T) + window_bias[None, :]
            raw_score = round_grad(content + relative_shift(positional)) * factor
            key_live = step_index * BLOCK + offsets < item_frames
            score_parts.append(jnp.where(key_live[None, :], raw_score, -1000000000.0))
            value_parts.append(value_rows)
        scores = jnp.concatenate(score_parts, axis=1)
        highest = jnp.max(scores, axis=1, keepdims=True)
        weights = jnp.exp(scores - highest)
        shares = weights / jnp.sum(weights, axis=1, keepdims=True)
        return product(round_value(shares), jnp.concatenate(value_parts, axis=0))

    blocks_out = lax.map(jax.checkpoint(one_block), jnp.arange(block_count, dtype=jnp.int32))
    return blocks_out.reshape(frames, queries.shape[1])


def all_heads(
    queries, keys_all, values_all, content_bias, position_bias, relative, item_start, item_length
):
    heads_here = queries.shape[1] // HEAD_DIM

    def split_heads(matrix):
        return matrix.reshape(matrix.shape[0], heads_here, HEAD_DIM).transpose(1, 0, 2)

    def per_head(pieces):
        return attend_head(
            pieces[0],
            pieces[1],
            pieces[2],
            pieces[3],
            pieces[4],
            pieces[5],
            item_start,
            item_length,
        )

    result = lax.map(
        per_head,
        (
            split_heads(queries),
            split_heads(keys_all),
            split_heads(values_all),
            content_bias.reshape(heads_here, HEAD_DIM),
            position_bias.reshape(heads_here, HEAD_DIM),
            split_heads(relative),
        ),
    )
    return result.transpose(1, 0, 2).reshape(queries.shape[0], heads_here * HEAD_DIM)


def feed_forward(values, norm_gain, in_weight, out_weight):
    hidden = round_value(layer_norm(values, norm_gain))
    gate_pre = round_grad(product(hidden, in_weight))
    active = round_value(jax.nn.silu(gate_pre))
    return 0.5 * round_grad(product(active, out_weight))


def attention_inputs(values, norm_gain, query_weight, key_weight, value_weight):
    hidden = round_value(layer_norm(values, norm_gain))
    return (
        round_grad(round_value(product(hidden, query_weight))),
        round_grad(round_value(product(hidden, key_weight))),
        round_grad(round_value(product(hidden, value_weight))),
    )


def attention_output(mixed_in, out_weight):
    return round_grad(product(mixed_in, out_weight))


def conv_inputs(values, norm_gain, wide_weight, live_mask):
    hidden = round_value(layer_norm(values, norm_gain))
    doubled = round_grad(product(hidden, wide_weight))
    half_width = doubled.shape[1] // 2
    gated = doubled[:, :half_width] * jax.nn.sigmoid(doubled[:, half_width:])
    return round_value(gated * live_mask[:, None])


def depthwise(extended, kernel, same_mask):
    half_taps = (TAPS - 1) // 2
    extent = extended.shape[0] - 2 * half_taps
    result = jnp.zeros((extent, extended.shape[1]), jnp.float32)
    for tap_index in range(TAPS):
        result = (
            result
            + kernel[tap_index]
            * extended[tap_index : tap_index + extent]
            * same_mask[half_taps : half_taps + extent, tap_index : tap_index + 1]
        )
    return result


def depthwise_back(extended, kernel, same_mask):
    half_taps = (TAPS - 1) // 2
    extent = extended.shape[0] - 2 * half_taps
    result = jnp.zeros((extent, extended.shape[1]), jnp.float32)
    for tap_index in range(TAPS):
        anchor = 2 * half_taps - tap_index
        result = (
            result
            + kernel[tap_index]
            * extended[anchor : anchor + extent]
            * same_mask[anchor : anchor + extent, tap_index : tap_index + 1]
        )
    return result


def kernel_grad(grad_rows, extended, same_mask):
    half_taps = (TAPS - 1) // 2
    extent = grad_rows.shape[0]
    sums = [
        jnp.sum(
            grad_rows
            * extended[tap_index : tap_index + extent]
            * same_mask[half_taps : half_taps + extent, tap_index : tap_index + 1],
            axis=0,
        )
        for tap_index in range(TAPS)
    ]
    return jnp.stack(sums, axis=0)


def conv_outputs(depth_in, norm_gain, out_weight):
    active = round_value(jax.nn.silu(layer_norm(depth_in, norm_gain)))
    return round_grad(product(active, out_weight))


def widen(members):
    return tuple((member.astype(jnp.float32) for member in members))


def gather_ffn(norm_gain, in_weight, out_weight):
    return (
        lax.all_gather(norm_gain, ("items", "seq"), axis=0, tiled=True),
        lax.all_gather(in_weight, ("items", "seq"), axis=0, tiled=True),
        lax.all_gather(out_weight, ("items", "seq"), axis=0, tiled=True),
    )


def body(
    features,
    item_spans,
    item_lengths,
    ffn1_gain,
    ffn1_in,
    ffn1_out,
    att_gain,
    w_query,
    w_key,
    w_value,
    w_pos,
    u_bias,
    v_bias,
    w_out,
    conv_gain,
    conv_in,
    depth_kernel,
    inner_gain,
    conv_out,
    ffn2_gain,
    ffn2_in,
    ffn2_out,
    final_gain,
    cotangent,
):
    seq_count = lax.axis_size("seq")
    seq_index = lax.axis_index("seq")
    tokens = features.shape[1]
    model_width = features.shape[2]
    frames = tokens * seq_count
    half_taps = (TAPS - 1) // 2
    item_start, item_length = block_layout(item_spans[0], item_lengths[0])
    first_frame = seq_index * tokens
    owners_wide, unused_valid = frame_items(
        first_frame - 2 * half_taps + jnp.arange(tokens + 4 * half_taps, dtype=jnp.int32),
        item_start,
        item_length,
        frames,
    )
    same_mask = same_item(owners_wide, tokens + 2 * half_taps)
    unused_owner, valid_frame = frame_items(
        first_frame + jnp.arange(tokens, dtype=jnp.int32), item_start, item_length, frames
    )
    live_mask = valid_frame.astype(jnp.float32)
    table_low = round_value(relative_table(model_width))
    stream = features[0]
    ffn1_set = widen(gather_ffn(ffn1_gain, ffn1_in, ffn1_out))
    branch_one, pull_one = jax.vjp(feed_forward, stream, ffn1_set[0], ffn1_set[1], ffn1_set[2])
    first = stream + branch_one
    att_set = widen(
        (
            lax.all_gather(att_gain, ("items", "seq"), axis=0, tiled=True),
            lax.all_gather(w_query, ("items", "seq"), axis=0, tiled=True),
            lax.all_gather(w_key, ("items", "seq"), axis=0, tiled=True),
            lax.all_gather(w_value, ("items", "seq"), axis=0, tiled=True),
            lax.all_gather(w_pos, ("items", "seq"), axis=0, tiled=True),
            lax.all_gather(u_bias, ("items", "seq"), axis=0, tiled=True),
            lax.all_gather(v_bias, ("items", "seq"), axis=0, tiled=True),
            lax.all_gather(w_out, ("items", "seq"), axis=0, tiled=True),
            lax.all_gather(final_gain, ("items", "seq"), axis=0, tiled=True),
        )
    )
    gain_att, query_full, key_full, value_full, pos_full, u_full, v_full, out_full, gain_last = (
        att_set
    )
    projected, pull_inputs = jax.vjp(
        attention_inputs, first, gain_att, query_full, key_full, value_full
    )
    heads_q, heads_k, heads_v = (
        lax.all_to_all(
            projected[0].astype(jnp.bfloat16), "seq", split_axis=1, concat_axis=0, tiled=True
        ),
        lax.all_to_all(
            projected[1].astype(jnp.bfloat16), "seq", split_axis=1, concat_axis=0, tiled=True
        ),
        lax.all_to_all(
            projected[2].astype(jnp.bfloat16), "seq", split_axis=1, concat_axis=0, tiled=True
        ),
    )
    slice_width = model_width // seq_count
    offset = seq_index * slice_width
    u_slice = lax.dynamic_slice_in_dim(u_full, offset, slice_width, 0)
    v_slice = lax.dynamic_slice_in_dim(v_full, offset, slice_width, 0)
    pos_slice = lax.dynamic_slice_in_dim(pos_full, offset, slice_width, 1)

    def head_piece(queries, keys_all, values_all, content_bias, position_bias, pos_columns):
        relative = round_grad(round_value(product(table_low, pos_columns)))
        return round_grad(
            round_value(
                all_heads(
                    queries,
                    keys_all,
                    values_all,
                    content_bias,
                    position_bias,
                    relative,
                    item_start,
                    item_length,
                )
            )
        )

    mixed_heads, pull_heads = jax.vjp(
        head_piece,
        heads_q.astype(jnp.float32),
        heads_k.astype(jnp.float32),
        heads_v.astype(jnp.float32),
        u_slice,
        v_slice,
        pos_slice,
    )
    mixed_frames = lax.all_to_all(
        mixed_heads.astype(jnp.bfloat16), "seq", split_axis=0, concat_axis=1, tiled=True
    )
    branch_two, pull_out = jax.vjp(attention_output, mixed_frames.astype(jnp.float32), out_full)
    second = first + branch_two
    conv_set = widen(
        (
            lax.all_gather(conv_gain, ("items", "seq"), axis=0, tiled=True),
            lax.all_gather(conv_in, ("items", "seq"), axis=0, tiled=True),
            lax.all_gather(depth_kernel, ("items", "seq"), axis=1, tiled=True),
            lax.all_gather(inner_gain, ("items", "seq"), axis=0, tiled=True),
            lax.all_gather(conv_out, ("items", "seq"), axis=0, tiled=True),
        )
    )
    gain_conv, wide_conv, kernel_full, gain_inner, proj_conv = conv_set

    def conv_front(values, norm_gain, wide_weight):
        return conv_inputs(values, norm_gain, wide_weight, live_mask)

    glu_out, pull_front = jax.vjp(conv_front, second, gain_conv, wide_conv)
    extended = padded(glu_out.astype(jnp.bfloat16), (("seq", 0),), 15).astype(jnp.float32)
    depth_out = depthwise(extended, kernel_full, same_mask)
    branch_three, pull_conv_back = jax.vjp(conv_outputs, depth_out, gain_inner, proj_conv)
    third = second + branch_three
    ffn2_set = widen(gather_ffn(ffn2_gain, ffn2_in, ffn2_out))
    branch_four, pull_four = jax.vjp(feed_forward, third, ffn2_set[0], ffn2_set[1], ffn2_set[2])
    fourth = third + branch_four
    layer_out, pull_final = jax.vjp(layer_norm, fourth, gain_last)
    grad_fourth, grad_final = pull_final(cotangent[0])
    grad_ffn2 = pull_four(grad_fourth)
    summed_ffn2 = (grad_ffn2[1], grad_ffn2[2], grad_ffn2[3])
    grad_third = grad_fourth + grad_ffn2[0]
    grad_depth, grad_inner, grad_proj = pull_conv_back(grad_third)
    depth_low = grad_depth.astype(jnp.bfloat16)
    depth_ext = padded(depth_low, (("seq", 0),), 15).astype(jnp.float32)
    grad_glu = depthwise_back(depth_ext, kernel_full, same_mask)
    grad_kernel = kernel_grad(depth_low.astype(jnp.float32), extended, same_mask)
    grad_second_conv, grad_cgain, grad_wide = pull_front(grad_glu)
    summed_conv = (grad_cgain, grad_wide, grad_kernel, grad_inner, grad_proj)
    grad_second = grad_third + grad_second_conv
    grad_mixed, grad_outw = pull_out(grad_second)
    sent_back = lax.all_to_all(
        grad_mixed.astype(jnp.bfloat16), "seq", split_axis=1, concat_axis=0, tiled=True
    )
    grad_hq, grad_hk, grad_hv, grad_u, grad_v, grad_pos = pull_heads(sent_back.astype(jnp.float32))
    returned = (
        lax.all_to_all(
            grad_hq.astype(jnp.bfloat16), "seq", split_axis=0, concat_axis=1, tiled=True
        ),
        lax.all_to_all(
            grad_hk.astype(jnp.bfloat16), "seq", split_axis=0, concat_axis=1, tiled=True
        ),
        lax.all_to_all(
            grad_hv.astype(jnp.bfloat16), "seq", split_axis=0, concat_axis=1, tiled=True
        ),
    )
    grad_first_att, grad_again, grad_query, grad_key, grad_value = pull_inputs(
        tuple((member.astype(jnp.float32) for member in returned))
    )
    grad_u_full = lax.dynamic_update_slice(
        jnp.zeros((model_width,), jnp.float32), grad_u, (offset,)
    )
    grad_v_full = lax.dynamic_update_slice(
        jnp.zeros((model_width,), jnp.float32), grad_v, (offset,)
    )
    grad_pos_full = lax.dynamic_update_slice(
        jnp.zeros((model_width, model_width), jnp.float32), grad_pos, (jnp.int32(0), offset)
    )
    summed_att = (
        grad_again,
        grad_query,
        grad_key,
        grad_value,
        grad_pos_full,
        grad_u_full,
        grad_v_full,
        grad_outw,
        grad_final,
    )
    grad_first = grad_second + grad_first_att
    grad_ffn1 = pull_one(grad_first)
    input_grad = grad_first + grad_ffn1[0]
    summed = (
        lax.psum_scatter(grad_ffn1[1], ("items", "seq"), scatter_dimension=0, tiled=True),
        lax.psum_scatter(grad_ffn1[2], ("items", "seq"), scatter_dimension=0, tiled=True),
        lax.psum_scatter(grad_ffn1[3], ("items", "seq"), scatter_dimension=0, tiled=True),
        lax.psum_scatter(summed_att[0], ("items", "seq"), scatter_dimension=0, tiled=True),
        lax.psum_scatter(summed_att[1], ("items", "seq"), scatter_dimension=0, tiled=True),
        lax.psum_scatter(summed_att[2], ("items", "seq"), scatter_dimension=0, tiled=True),
        lax.psum_scatter(summed_att[3], ("items", "seq"), scatter_dimension=0, tiled=True),
        lax.psum_scatter(summed_att[4], ("items", "seq"), scatter_dimension=0, tiled=True),
        lax.psum_scatter(summed_att[5], ("items", "seq"), scatter_dimension=0, tiled=True),
        lax.psum_scatter(summed_att[6], ("items", "seq"), scatter_dimension=0, tiled=True),
        lax.psum_scatter(summed_att[7], ("items", "seq"), scatter_dimension=0, tiled=True),
        lax.psum_scatter(summed_conv[0], ("items", "seq"), scatter_dimension=0, tiled=True),
        lax.psum_scatter(summed_conv[1], ("items", "seq"), scatter_dimension=0, tiled=True),
        lax.psum_scatter(summed_conv[2], ("items", "seq"), scatter_dimension=1, tiled=True),
        lax.psum_scatter(summed_conv[3], ("items", "seq"), scatter_dimension=0, tiled=True),
        lax.psum_scatter(summed_conv[4], ("items", "seq"), scatter_dimension=0, tiled=True),
        lax.psum_scatter(summed_ffn2[0], ("items", "seq"), scatter_dimension=0, tiled=True),
        lax.psum_scatter(summed_ffn2[1], ("items", "seq"), scatter_dimension=0, tiled=True),
        lax.psum_scatter(summed_ffn2[2], ("items", "seq"), scatter_dimension=0, tiled=True),
        lax.psum_scatter(summed_att[8], ("items", "seq"), scatter_dimension=0, tiled=True),
    )
    return (
        layer_out[None],
        input_grad[None],
        summed[0],
        summed[1],
        summed[2],
        summed[3],
        summed[4],
        summed[5],
        summed[6],
        summed[7],
        summed[8],
        summed[9],
        summed[10],
        summed[11],
        summed[12],
        summed[13],
        summed[14],
        summed[15],
        summed[16],
        summed[17],
        summed[18],
        summed[19],
    )


def solution(mesh):
    placed = (
        P("items", "seq", None),
        P("items", None),
        P("items", None),
        P(("items", "seq")),
        P(("items", "seq"), None),
        P(("items", "seq"), None),
        P(("items", "seq")),
        P(("items", "seq"), None),
        P(("items", "seq"), None),
        P(("items", "seq"), None),
        P(("items", "seq"), None),
        P(("items", "seq")),
        P(("items", "seq")),
        P(("items", "seq"), None),
        P(("items", "seq")),
        P(("items", "seq"), None),
        P(None, ("items", "seq")),
        P(("items", "seq")),
        P(("items", "seq"), None),
        P(("items", "seq")),
        P(("items", "seq"), None),
        P(("items", "seq"), None),
        P(("items", "seq")),
        P("items", "seq", None),
    )
    return jax.shard_map(
        body,
        mesh=mesh,
        in_specs=placed,
        out_specs=(
            P("items", "seq", None),
            P("items", "seq", None),
            P(("items", "seq")),
            P(("items", "seq"), None),
            P(("items", "seq"), None),
            P(("items", "seq")),
            P(("items", "seq"), None),
            P(("items", "seq"), None),
            P(("items", "seq"), None),
            P(("items", "seq"), None),
            P(("items", "seq")),
            P(("items", "seq")),
            P(("items", "seq"), None),
            P(("items", "seq")),
            P(("items", "seq"), None),
            P(None, ("items", "seq")),
            P(("items", "seq")),
            P(("items", "seq"), None),
            P(("items", "seq")),
            P(("items", "seq"), None),
            P(("items", "seq"), None),
            P(("items", "seq")),
        ),
        check_vma=False,
    )
```

profile of v0, /device:TPU:0, one launch (start us, length us, event | category | flops | bytes accessed | tf_op | source)
XLA Modules:
  0.0 4937.2 jit_solution(14516869187535792673)
XLA Ops:
  20.7 42.8 all-reduce.25
  102.2 68.3 %all-gather.14.cloned.1.call-done = bf16[4096,1024]{1,0:T(8,128)(2,1)} async-done(((bf16[128,1024]{1,0:T(8,128)(2,1)}), bf16[4096,1024]{1,0:T(8,128)(2,1)}) %all-gather.14.cloned.1.call-update) | async-done | bytes 8388624 | tf_op jit(solution)/shard_map/all_gather | solution.py:305
  180.5 48.1 all-gather.18.cloned.1.call-done
  238.0 50.3 %all-gather.16.cloned.1.call-done = bf16[1024,1024]{1,0:T(8,128)(2,1)} async-done(((bf16[32,1024]{1,0:T(8,128)(2,1)}), bf16[1024,1024]{1,0:T(8,128)(2,1)}) %all-gather.16.cloned.1.call-update) | async-done | bytes 2097168 | tf_op jit(solution)/shard_map/all_gather | solution.py:362
  297.0 146.9 %while.202 = (s32[]{:T(128)}, s32[8]{0:T(128)}, s32[8]{0:T(128)}, s32[8]{0:T(128)}, pred[8,512,512]{1,2,0:T(32,128)(4,1)}, /*index=5*/s32[8]{0:T(128)}, s32[8]{0...) while((s32[]{:T(128)}, s32[8]{0:T(128)}, s32[8]{0:T(128)}, ...), condition=%wide.region_6.7_spmd.clone.clone, body=%wide.region_5.6_spmd.clone.sunk.clone | while | flops 2615 | bytes 791432 | solution.py:182
  445.4 24.6 fusion.101
  521.6 896.9 %while.201 = (s32[]{:T(128)}, bf16[2,4096,64]{1,2,0:T(8,128)(2,1)}, f32[2,1,64]{2,1,0:T(1,128)}, f32[2,1,64]{2,1,0:T(1,128)}, f32[2,4096]{1,0:T(2,128)}, /*index...) while((s32[]{:T(128)}, bf16[2,4096,64]{1,2,0:T(8,128)(2,1)}, ...), condition=%wide.region_16.17_spmd.clone, body=%wide.region_7.16_spmd.sunk.clone | while | flops 417193984 | bytes 126272288 | solution.py:206
  544.1 424.3 %while.200 = (s32[]{:T(128)}, bf16[8,512,64]{1,2,0:T(8,128)(2,1)}, pred[8,512,512]{1,2,0:T(32,128)(4,1)}, s32[8]{0:T(128)}, bf16[4096,64]{1,0:T(8,128)(2,1)}, /*...) while((s32[]{:T(128)}, bf16[8,512,64]{1,2,0:T(8,128)(2,1)}, ...), condition=%wide.region_15.15_spmd, body=%wide.region_10.14_spmd.sunk | while | flops 415824896 | bytes 82330152 | solution.py:182
  987.2 423.9 %while.200 = (s32[]{:T(128)}, bf16[8,512,64]{1,2,0:T(8,128)(2,1)}, pred[8,512,512]{1,2,0:T(32,128)(4,1)}, s32[8]{0:T(128)}, bf16[4096,64]{1,0:T(8,128)(2,1)}, /*...) while((s32[]{:T(128)}, bf16[8,512,64]{1,2,0:T(8,128)(2,1)}, ...), condition=%wide.region_15.15_spmd, body=%wide.region_10.14_spmd.sunk | while | flops 415824896 | bytes 82330152 | solution.py:182
  1427.3 55.7 %all_gather.71 = bf16[31,1024]{0,1:T(8,128)(2,1)S(1)} all-gather(bf16[31,32]{0,1:T(8,128)(2,1)S(1)} %copy.215), channel_id=1, replica_groups=mesh['items'=4,'seq'=8] {'items','seq'}, dimensions={1}, use_global_device_ids=true | all-gather | bytes 65472 | tf_op jit(solution)/shard_map/all_gather | solution.py:430
  1686.8 1758.1 %while.204 = (s32[]{:T(128)}, bf16[2,4096,64]{1,2,0:T(8,128)(2,1)}, bf16[2,4096,64]{1,2,0:T(8,128)(2,1)}, bf16[2,4096,64]{1,2,0:T(8,128)(2,1)}, f32[2,64]{1,0:T(...) while((s32[]{:T(128)}, bf16[2,4096,64]{1,2,0:T(8,128)(2,1)}, ...), condition=%wide.region_51.53_spmd.clone.clone, body=%wide.region_33.52_spmd.clone.sunk.clone | while | flops 1144667136 | bytes 292520704 | solution.py:206
  1718.7 843.5 %while.203 = (s32[]{:T(128)}, f32[4096,64]{0,1:T(8,128)}, f32[4096,64]{0,1:T(8,128)}, f32[4096,64]{0,1:T(8,128)}, f32[4096]{0:T(1024)}, /*index=5*/f32[3072,64]{...) while((s32[]{:T(128)}, f32[4096,64]{0,1:T(8,128)}, ...), condition=%wide.region_48.49_spmd.clone, body=%wide.region_34.48_spmd.clone.sunk | while | flops 1142832128 | bytes 235309872 | solution.py:182
  2584.3 843.0 %while.203 = (s32[]{:T(128)}, f32[4096,64]{0,1:T(8,128)}, f32[4096,64]{0,1:T(8,128)}, f32[4096,64]{0,1:T(8,128)}, f32[4096]{0:T(1024)}, /*index=5*/f32[3072,64]{...) while((s32[]{:T(128)}, f32[4096,64]{0,1:T(8,128)}, ...), condition=%wide.region_48.49_spmd.clone, body=%wide.region_34.48_spmd.clone.sunk | while | flops 1142832128 | bytes 235309872 | solution.py:182
  3454.8 39.0 all_to_all.125
  3499.0 38.3 all_to_all.126
  3542.5 39.5 all_to_all.127
  3674.3 37.8 all-reduce.24
  3744.4 142.1 %reduce-scatter.21.cloned.1.call-done = f32[32,1024]{1,0:T(8,128)} async-done(((f32[1024,1024]{1,0:T(8,128)}), f32[32,1024]{1,0:T(8,128)}) %reduce-scatter.21.cloned.1.call-update) | async-done | bytes 131088 | tf_op jit(solution)/shard_map/reduce_scatter | solution.py:509
  3886.6 141.9 %reduce-scatter.23.cloned.1.call-done = f32[32,1024]{1,0:T(8,128)} async-done(((f32[1024,1024]{1,0:T(8,128)}), f32[32,1024]{1,0:T(8,128)}) %reduce-scatter.23.cloned.1.call-update) | async-done | bytes 131088 | tf_op jit(solution)/shard_map/reduce_scatter | solution.py:510
  4028.5 152.6 %reduce-scatter.29.cloned.1.call-done = f32[32,2048]{1,0:T(8,128)} async-done(((f32[1024,2048]{1,0:T(8,128)}), f32[32,2048]{1,0:T(8,128)}) %reduce-scatter.29.cloned.1.call-update) | async-done | bytes 262160 | tf_op jit(solution)/shard_map/reduce_scatter | solution.py:516
  4181.0 187.1 %reduce-scatter.35.cloned.1.call-done = f32[128,1024]{1,0:T(8,128)} async-done(((f32[4096,1024]{1,0:T(8,128)}), f32[128,1024]{1,0:T(8,128)}) %reduce-scatter.35.cloned.1.call-update) | async-done | bytes 524304 | tf_op jit(solution)/shard_map/reduce_scatter | solution.py:522
  4368.2 187.4 %reduce-scatter.33.cloned.1.call-done = f32[32,4096]{1,0:T(8,128)} async-done(((f32[1024,4096]{1,0:T(8,128)}), f32[32,4096]{1,0:T(8,128)}) %reduce-scatter.33.cloned.1.call-update) | async-done | bytes 524304 | tf_op jit(solution)/shard_map/reduce_scatter | solution.py:521
  4555.5 187.3 %reduce-scatter.17.cloned.1.call-done = f32[128,1024]{1,0:T(8,128)} async-done(((f32[4096,1024]{1,0:T(8,128)}), f32[128,1024]{1,0:T(8,128)}) %reduce-scatter.17.cloned.1.call-update) | async-done | bytes 524304 | tf_op jit(solution)/shard_map/reduce_scatter | solution.py:506
  4742.9 187.4 %reduce-scatter.15.cloned.1.call-done = f32[32,4096]{1,0:T(8,128)} async-done(((f32[1024,4096]{1,0:T(8,128)}), f32[32,4096]{1,0:T(8,128)}) %reduce-scatter.15.cloned.1.call-update) | async-done | bytes 524304 | tf_op jit(solution)/shard_map/reduce_scatter | solution.py:505
  (3892 shorter events, 3099.7 us)
Async XLA Ops:
  7.2 84.0 %all-gather.12.cloned.1.call-start = ((), (), s32[]{:S(2)}) async-start(), calls=%async_computation.20 | async-start | bytes 8650752 | tf_op jit(solution)/shard_map/all_gather | solution.py:304
  8.0 162.5 %all-gather.14.cloned.1.call-start = ((), (), s32[]{:S(2)}) async-start(), calls=%async_computation.21 | async-start | bytes 8650752 | tf_op jit(solution)/shard_map/all_gather | solution.py:305
  8.7 219.9 %all-gather.18.cloned.1.call-start = ((), (), s32[]{:S(2)}) async-start(), calls=%async_computation.23 | async-start | bytes 2162688 | tf_op jit(solution)/shard_map/all_gather | solution.py:363
  9.4 278.9 %all-gather.16.cloned.1.call-start = ((), (), s32[]{:S(2)}) async-start(), calls=%async_computation.22 | async-start | bytes 2162688 | tf_op jit(solution)/shard_map/all_gather | solution.py:362
  10.0 460.0 %all-gather.20.cloned.1.call-start = ((), (), s32[]{:S(2)}) async-start(), calls=%async_computation.24 | async-start | bytes 2162688 | tf_op jit(solution)/shard_map/all_gather | solution.py:364
  10.6 483.7 %all-gather.22.cloned.1.call-start = ((), (), s32[]{:S(2)}) async-start(), calls=%async_computation.25 | async-start | bytes 2162688 | tf_op jit(solution)/shard_map/all_gather | solution.py:365
  11.2 1490.4 %all-gather.24.cloned.1.call-start = ((), (), s32[]{:S(2)}) async-start(), calls=%async_computation.26 | async-start | bytes 2162688 | tf_op jit(solution)/shard_map/all_gather | solution.py:368
  11.9 1494.7 %all-gather.26.cloned.1.call-start = ((), (), s32[]{:S(2)}) async-start(), calls=%async_computation.27 | async-start | bytes 4325376 | tf_op jit(solution)/shard_map/all_gather | solution.py:429
  12.7 1522.8 %all-gather.28.cloned.1.call-start = ((), (), s32[]{:S(2)}) async-start(), calls=%async_computation.28 | async-start | bytes 2162688 | tf_op jit(solution)/shard_map/all_gather | solution.py:432
  13.4 1528.3 %all-gather.30.cloned.1.call-start = ((), (), s32[]{:S(2)}) async-start(), calls=%async_computation.29 | async-start | bytes 8650752 | tf_op jit(solution)/shard_map/all_gather | solution.py:304
  236.3 1316.9 %all-gather.32.cloned.1.call-start = ((), (), s32[]{:S(2)}) async-start(), calls=%async_computation.30 | async-start | bytes 8650752 | tf_op jit(solution)/shard_map/all_gather | solution.py:305
  292.5 184.0 %all-to-all-start = ((bf16[512,8,128]{0,2,1:T(8,128)(2,1)}), bf16[512,8,128]{0,2,1:T(8,128)(2,1)}, u32[]{:S(2)}, u32[]{:S(2)}) async-start(bf16[512,8,128]{0,2,1:T(8,128)(2,1)} %bitcast.23), calls=%async_computation | async-start | bytes 2097152 | tf_op jit(solution)/shard_map/all_to_all | solution.py:379
  1426.1 2235.1 %reduce-scatter.37.cloned.1.call-start = ((), (), s32[]{:S(2)}) async-start(), calls=%async_computation.42 | async-start | bytes 540672
  1612.2 2108.6 %reduce-scatter.31.cloned.1.call-start = ((), (), s32[]{:S(2)}) async-start(), calls=%async_computation.39 | async-start | bytes 4325376 | tf_op jit(solution)/shard_map/reduce_scatter | solution.py:519
  1652.4 2068.4 %reduce-scatter.27.cloned.1.call-start = ((), (), s32[]{:S(2)}) async-start(), calls=%async_computation.37 | async-start | bytes 4325376 | tf_op jit(solution)/shard_map/reduce_scatter | solution.py:514
  1656.9 2063.9 %reduce-scatter.25.cloned.1.call-start = ((), (), s32[]{:S(2)}) async-start(), calls=%async_computation.36 | async-start | bytes 4325376 | tf_op jit(solution)/shard_map/reduce_scatter | solution.py:511
  3452.9 291.5 %reduce-scatter.19.cloned.1.call-start = ((), (), s32[]{:S(2)}) async-start(), calls=%async_computation.33 | async-start | bytes 4325376 | tf_op jit(solution)/shard_map/reduce_scatter | solution.py:508
  3497.1 389.4 %reduce-scatter.21.cloned.1.call-start = ((), (), s32[]{:S(2)}) async-start(), calls=%async_computation.34 | async-start | bytes 4325376 | tf_op jit(solution)/shard_map/reduce_scatter | solution.py:509
  3540.6 487.8 %reduce-scatter.23.cloned.1.call-start = ((), (), s32[]{:S(2)}) async-start(), calls=%async_computation.35 | async-start | bytes 4325376 | tf_op jit(solution)/shard_map/reduce_scatter | solution.py:510
  3585.3 595.7 %reduce-scatter.29.cloned.1.call-start = ((), (), s32[]{:S(2)}) async-start(), calls=%async_computation.38 | async-start | bytes 8650752 | tf_op jit(solution)/shard_map/reduce_scatter | solution.py:516
  3593.9 774.3 %reduce-scatter.35.cloned.1.call-start = ((), (), s32[]{:S(2)}) async-start(), calls=%async_computation.41 | async-start | bytes 17301504 | tf_op jit(solution)/shard_map/reduce_scatter | solution.py:522
  3605.7 949.8 %reduce-scatter.33.cloned.1.call-start = ((), (), s32[]{:S(2)}) async-start(), calls=%async_computation.40 | async-start | bytes 17301504 | tf_op jit(solution)/shard_map/reduce_scatter | solution.py:521
  3617.3 1125.5 %reduce-scatter.17.cloned.1.call-start = ((), (), s32[]{:S(2)}) async-start(), calls=%async_computation.32 | async-start | bytes 17301504 | tf_op jit(solution)/shard_map/reduce_scatter | solution.py:506
  3639.5 1290.7 %reduce-scatter.15.cloned.1.call-start = ((), (), s32[]{:S(2)}) async-start(), calls=%async_computation.31 | async-start | bytes 17301504 | tf_op jit(solution)/shard_map/reduce_scatter | solution.py:505
  (763 other events, 5786.8 us)
Sparse Core Ops, SparseCore 0:
  11.0 80.0 all-gather.11
  94.2 76.2 all-gather.13
  173.5 55.0 all-gather.17
  231.4 56.8 all-gather.15
  291.1 56.5 all-gather.19
  350.6 55.3 all-gather.21
  409.0 55.3 all-gather.23
  467.4 70.3 all-gather.25
  540.8 55.0 all-gather.27
  598.7 76.2 all-gather.29
  678.0 75.9 all-gather.31
  1612.3 133.4 reduce-scatter.36
  1748.7 138.9 reduce-scatter.30
  1890.6 139.6 reduce-scatter.26
  3453.0 147.4 reduce-scatter.24
  3603.3 141.0 reduce-scatter.18
  3747.2 139.2 reduce-scatter.20
  3889.4 139.0 reduce-scatter.22
  4031.4 149.5 reduce-scatter.28
  4183.9 184.2 reduce-scatter.34
  4371.2 184.3 reduce-scatter.32
  4558.5 184.3 reduce-scatter.16
  4745.8 184.3 reduce-scatter.14
where the time goes:
time: 4970 us; the launch traced here: 4940 us
  local copies, waits for them, and re-layouts  1840 us (37%)
  waiting for transfers between devices  1430 us (29%)
  matrix products  863 us (17%)
  other arithmetic  308 us (6%)
  blocking collectives  253 us (5%)
  loops' own time  190 us (4%)
    dot_general x453, matrix products, product(): return make_low_product()(left_side, right_side)  796 us
    reshape x144, local copies, waits for them, and re-layouts, relative_shift(): return diagonal_band.reshape(BLOCK, 2 * BLOCK - 1)[:, :BLOCK]  496 us
    reduce_scatter x1, waiting for transfers between devices, body(): lax.psum_scatter(grad_ffn1[2], ('items', 'seq'), scatter_dimension=0, til...  187 us
    reduce_scatter x1, waiting for transfers between devices, body(): lax.psum_scatter(summed_ffn2[1], ('items', 'seq'), scatter_dimension=0, t...  187 us
    reduce_scatter x1, waiting for transfers between devices, body(): lax.psum_scatter(grad_ffn1[3], ('items', 'seq'), scatter_dimension=0, til...  187 us
    reduce_scatter x1, waiting for transfers between devices, body(): lax.psum_scatter(summed_ffn2[2], ('items', 'seq'), scatter_dimension=0, t...  187 us
    while x1316, local copies, waits for them, and re-layouts  162 us
    dynamic_slice x136, local copies, waits for them, and re-layouts, attend_head(): lax.map(jax.checkpoint(one_block), jnp.arange(block_count, dtype=jnp.int32))  155 us
  transfers between devices with their start and end apart: 32, of which 14 were waited for; matrix products, arithmetic and copies ran while one was open for 57% of the time, Pallas kernels for 0%

commit v1 on v0

v1 whole, which is shorter than its diff:
```python
import functools
import math

import jax
import jax.numpy as jnp
from jax import lax
from jax.experimental import pallas as pl
from jax.experimental.pallas import tpu as pltpu
from jax.sharding import PartitionSpec as P

HEAD_DIM = 64
TAPS = 31
BLOCK = 512
HALF = (TAPS - 1) // 2
EPSILON = 1e-05
NEAR = 3
KEYS = NEAR * BLOCK
RELS = 4 * BLOCK
LANES = 128
ROWS = 128
WINDOW = KEYS + LANES
BF = jnp.bfloat16
F32 = jnp.float32
AXES = ("items", "seq")
SMALL = 128


def dot(left, right):
    return jnp.dot(left, right, preferred_element_type=F32)


def dot_nt(left, right):
    return lax.dot_general(left, right, (((1,), (1,)), ((), ())), preferred_element_type=F32)


def dot_tn(left, right):
    return lax.dot_general(left, right, (((0,), (0,)), ((), ())), preferred_element_type=F32)


def tile_cut(group):
    near = LANES - 4 - 8 * group
    upper = lax.broadcasted_iota(jnp.int32, (8, LANES), 0) < 4
    lane = lax.broadcasted_iota(jnp.int32, (8, LANES), 1)
    return near, near - 4, upper, lane


def own_lanes(half):
    return lax.broadcasted_iota(jnp.int32, (1, LANES), 1) // HEAD_DIM == half


def twice(values, own):
    return jnp.where(own, values, pltpu.roll(values, HEAD_DIM, 1))


def slotted(values):
    row = lax.broadcasted_iota(jnp.int32, values.shape, 0)
    slot = lax.broadcasted_iota(jnp.int32, values.shape, 1) // HEAD_DIM
    place = 3 - row % 4
    return jnp.concatenate(
        [jnp.where(slot == place, values, 0.0), jnp.where(slot + 2 == place, values, 0.0)], axis=1
    ).astype(BF)


def four_rows(r_ref, r_scr, own):
    r_scr[0:RELS, :] = twice(r_ref[...].astype(F32), own)
    r_scr[RELS : RELS + 8, :] = jnp.zeros((8, LANES), F32)
    low = lax.broadcasted_iota(jnp.int32, (1, LANES), 1) < HEAD_DIM
    return jnp.concatenate(
        [
            jnp.where(low, r_scr[s : s + RELS, :], r_scr[s + 1 : s + 1 + RELS, :]).astype(BF)
            for s in (0, 2)
        ],
        axis=1,
    )


def positions_kernel(q_ref, r_ref, b_ref, out_ref, pos_scr, r_scr):
    own = own_lanes(pl.program_id(1))
    qb = (q_ref[...].astype(F32) + b_ref[...].astype(F32)) * HEAD_DIM**-0.5
    pos_scr[...] = dot_nt(slotted(twice(qb, own)), four_rows(r_ref, r_scr, own))

    def chunk(c, carry):
        first = (BLOCK // ROWS - 1 - c) * LANES
        for group in range(ROWS // 8):
            rows = pl.ds(pl.multiple_of(c * ROWS + 8 * group, 8), 8)
            near, far, upper, lane = tile_cut(group)
            stay = lane < LANES - jnp.where(upper, near, far)
            before = None
            for j in range(WINDOW // LANES):
                tile = pos_scr[rows, pl.ds(pl.multiple_of(first + j * LANES, LANES), LANES)]
                moved = jnp.where(
                    upper,
                    pltpu.roll(tile, LANES - near, 1),
                    pltpu.roll(tile, LANES - far, 1) if far else tile,
                )
                if j:
                    out_ref[0, rows, (j - 1) * LANES : j * LANES] = jnp.where(stay, before, moved)
                before = moved
        return carry

    lax.fori_loop(0, BLOCK // ROWS, chunk, 0)


def attend_kernel(
    live_ref, q_ref, k_ref, v_ref, u_ref, pos_ref, mix_ref, e_ref, inv_ref, s_scr, sum_scr, top_scr
):
    half = pl.program_id(1)
    own = own_lanes(half)
    scale = HEAD_DIM**-0.5
    q = q_ref[...].astype(F32)
    qm = jnp.where(own, q * scale, 0.0).astype(BF)
    um = jnp.broadcast_to(jnp.where(own, u_ref[...].astype(F32) * scale, 0.0), q.shape).astype(BF)
    k = k_ref[...]
    s_scr[...] = dot_nt(jnp.concatenate([qm, um], axis=1), jnp.concatenate([k, k], axis=1))
    keep = lax.broadcasted_iota(jnp.int32, (1, KEYS), 1) < live_ref[0]
    mask = jnp.where(keep, 0.0, -1000000000.0)

    def chunk(c, carry):
        for group in range(ROWS // 8):
            rows = pl.ds(pl.multiple_of(c * ROWS + 8 * group, 8), 8)
            top = None
            for j in range(KEYS // LANES):
                at = slice(j * LANES, (j + 1) * LANES)
                score = s_scr[rows, at] + mask[:, at] + pos_ref[0, rows, at]
                sum_scr[rows, at] = score
                top = score if top is None else jnp.maximum(top, score)
            top_scr[8 * group : 8 * group + 8, :] = top
        tops = jnp.max(top_scr[...], axis=1, keepdims=True)
        for pair in range(ROWS // 16):
            rows = pl.ds(pl.multiple_of(c * ROWS + 16 * pair, 16), 16)
            e_ref[0, rows, :] = jnp.exp(sum_scr[rows, :] - tops[16 * pair : 16 * pair + 16]).astype(BF)
        return carry

    lax.fori_loop(0, BLOCK // ROWS, chunk, 0)
    ones = jnp.where(own, v_ref[...].astype(F32), 1.0).astype(BF)
    both = dot(e_ref[0], ones)
    inverse = 1.0 / pltpu.roll(both, HEAD_DIM, 1)
    mixed = both * inverse

    @pl.when(half == 0)
    def _():
        mix_ref[...] = mixed.astype(BF)
        inv_ref[...] = inverse

    @pl.when(half == 1)
    def _():
        mix_ref[...] = jnp.where(own, mixed, mix_ref[...].astype(F32)).astype(BF)
        inv_ref[...] = jnp.where(own, inverse, inv_ref[...])


def pair_block(rows):
    return pl.BlockSpec((rows, LANES), lambda i, h: (0, i))


def head_block(frames):
    return pl.BlockSpec((1, frames, KEYS), lambda i, h: (2 * i + h, 0, 0))


def heads_call(kernel, name, ins, outs, scratch, flops, exps=0):
    pairs = next(a.shape[1] for a, _ in ins if a.ndim == 2) // LANES
    moved = sum(math.prod(a.shape) * a.dtype.itemsize for a, _ in ins)
    moved += sum(math.prod(shape) * jnp.dtype(dtype).itemsize for shape, dtype, _ in outs)
    return pl.pallas_call(
        kernel,
        grid=(pairs, 2),
        in_specs=[spec for _, spec in ins],
        out_specs=[spec for _, _, spec in outs],
        out_shape=[jax.ShapeDtypeStruct(shape, dtype) for shape, dtype, _ in outs],
        scratch_shapes=[pltpu.VMEM(shape, dtype) for shape, dtype in scratch],
        compiler_params=pltpu.CompilerParams(vmem_limit_bytes=48 * 1024 * 1024),
        cost_estimate=pl.CostEstimate(
            flops=8 * flops * 2 * pairs, bytes_accessed=moved, transcendentals=exps * 2 * pairs
        ),
        name=name,
    )(*[a for a, _ in ins])


def relative_scores(q, rel, b):
    frames, width = q.shape
    return heads_call(
        positions_kernel,
        "positions",
        [(q, pair_block(frames)), (rel, pair_block(RELS)), (b, pair_block(1))],
        [((width // HEAD_DIM, frames, KEYS), F32, head_block(frames))],
        [((frames, RELS), F32), ((RELS + 8, LANES), F32)],
        frames * RELS * LANES,
    )[0]


def attend(live, q, k, v, u, relative):
    frames, width = q.shape
    return heads_call(
        attend_kernel,
        "attend",
        [
            (live, pl.BlockSpec(memory_space=pltpu.SMEM)),
            (q, pair_block(frames)),
            (k, pair_block(KEYS)),
            (v, pair_block(KEYS)),
            (u, pair_block(1)),
            (relative, head_block(frames)),
        ],
        [
            ((frames, width), BF, pair_block(frames)),
            ((width // HEAD_DIM, frames, KEYS), BF, head_block(frames)),
            ((frames, width), F32, pair_block(frames)),
        ],
        [((frames, KEYS), F32), ((frames, KEYS), F32), ((ROWS, LANES), F32)],
        2 * frames * KEYS * LANES,
        frames * KEYS,
    )


def keys_back_kernel(
    q_ref, v_ref, u_ref, g_ref, mix_ref, inv_ref, e_ref, ds_ref, dk_ref, dv_ref, dp_scr
):
    frames = q_ref.shape[0]
    qu = (q_ref[...].astype(F32) + u_ref[...].astype(F32)) * HEAD_DIM**-0.5
    grad = g_ref[...].astype(F32) * inv_ref[...]
    lane = lax.broadcasted_iota(jnp.int32, (1, LANES), 1)
    minus = jnp.broadcast_to(jnp.where(lane < 2, -1.0, 0.0), (KEYS, LANES)).astype(BF)
    wide_v = jnp.concatenate([v_ref[...], minus], axis=1)
    qus, gms = [], []
    for half in range(2):
        own = own_lanes(half)
        qus.append(jnp.where(own, qu, 0.0).astype(BF))
        gm = jnp.where(own, grad, 0.0).astype(BF)
        total = jnp.sum(gm.astype(F32) * mix_ref[...].astype(F32), axis=1, keepdims=True)
        high = total.astype(BF).astype(F32)
        totals = jnp.where(lane == 0, high, jnp.where(lane == 1, total - high, 0.0)).astype(BF)
        dp_scr[half] = dot_nt(jnp.concatenate([gm, totals], axis=1), wide_v)
        gms.append(gm)
    gm = jnp.concatenate(gms, axis=0)
    both = e_ref[...].reshape(2 * frames, KEYS)
    dv_ref[...] = dot_tn(gm, both).T.astype(BF)

    def chunk(c, carry):
        rows = pl.ds(pl.multiple_of(c * ROWS, ROWS), ROWS)
        for half in range(2):
            for j in range(KEYS // LANES):
                at = slice(j * LANES, (j + 1) * LANES)
                ds_ref[half, rows, at] = (
                    e_ref[half, rows, at].astype(F32) * dp_scr[half, rows, at]
                ).astype(BF)
        return carry

    lax.fori_loop(0, frames // ROWS, chunk, 0)
    dk_t = dot_tn(jnp.concatenate(qus, axis=0), ds_ref[...].reshape(2 * frames, KEYS))
    dk_ref[...] = dk_t.T.astype(BF)


def pairs_call(kernel, name, ins, outs, scratch, flops):
    pairs = ins[0][0].shape[1] // LANES

    def spec(shape, rows):
        if rows:
            return pl.BlockSpec((rows, LANES), lambda i: (0, i))
        return pl.BlockSpec((2, *shape[1:]), lambda i: (i, 0, 0))

    moved = sum(math.prod(a.shape) * a.dtype.itemsize for a, _ in ins)
    moved += sum(math.prod(shape) * jnp.dtype(dtype).itemsize for shape, dtype, _ in outs)
    return pl.pallas_call(
        kernel,
        grid=(pairs,),
        in_specs=[spec(a.shape, rows) for a, rows in ins],
        out_specs=[spec(shape, rows) for shape, _, rows in outs],
        out_shape=[jax.ShapeDtypeStruct(shape, dtype) for shape, dtype, _ in outs],
        scratch_shapes=[pltpu.VMEM(shape, dtype) for shape, dtype in scratch],
        compiler_params=pltpu.CompilerParams(vmem_limit_bytes=56 * 1024 * 1024),
        cost_estimate=pl.CostEstimate(
            flops=16 * flops * pairs, bytes_accessed=moved, transcendentals=0
        ),
        name=name,
    )(*[a for a, _ in ins])


def keys_back(q, v, u, grad, mixed, inverse, weights):
    frames, width = q.shape
    return pairs_call(
        keys_back_kernel,
        "keys_back",
        [
            (q, frames),
            (v, KEYS),
            (u, 1),
            (grad, frames),
            (mixed, frames),
            (inverse, frames),
            (weights, 0),
        ],
        [
            ((width // HEAD_DIM, frames, KEYS), BF, 0),
            ((KEYS, width), BF, KEYS),
            ((KEYS, width), BF, KEYS),
        ],
        [((2, frames, KEYS), F32)],
        3 * frames * KEYS * LANES,
    )


def unskew(ds_ref, dun_scr, half, c):
    first = (BLOCK // ROWS - 1 - c) * LANES
    for pair in range(ROWS // 16):
        rows = pl.ds(pl.multiple_of(c * ROWS + 16 * pair, 16), 16)
        before = [jnp.zeros((8, LANES), F32)] * 2
        for j in range(WINDOW // LANES):
            outs = []
            if j < KEYS // LANES:
                scores = ds_ref[half, rows, j * LANES : (j + 1) * LANES].astype(F32)
            for part in range(2):
                near, far, upper, lane = tile_cut(2 * pair + part)
                if j < KEYS // LANES:
                    score = scores[8 * part : 8 * part + 8]
                    moved = jnp.where(
                        upper,
                        pltpu.roll(score, near, 1),
                        pltpu.roll(score, far, 1) if far else score,
                    )
                else:
                    moved = jnp.zeros((8, LANES), F32)
                outs.append(jnp.where(lane >= jnp.where(upper, near, far), moved, before[part]))
                before[part] = moved
            there = pl.ds(pl.multiple_of(first + j * LANES, LANES), LANES)
            dun_scr[rows, there] = jnp.concatenate(outs, axis=0).astype(BF)


def queries_back_kernel(
    q_ref, k_ref, r_ref, b_ref, ds_ref, dq_ref, dr_ref, du_ref, db_ref,
    dun0_scr, dun1_scr, r_scr, rc_scr, dqk_scr, wide_scr, four_scr,
):
    scale = HEAD_DIM**-0.5
    frames = q_ref.shape[0]
    duns = (dun0_scr, dun1_scr)
    part = RELS // (BLOCK // ROWS)

    @pl.when(pl.program_id(0) == 0)
    def _():
        dun0_scr[...] = jnp.zeros_like(dun0_scr)
        dun1_scr[...] = jnp.zeros_like(dun1_scr)

    qb = (q_ref[...].astype(F32) + b_ref[...].astype(F32)) * scale
    qbs = [slotted(twice(qb, own_lanes(half))) for half in range(2)]
    rc_scr[...] = four_rows(r_ref, r_scr, own_lanes(0))
    k = k_ref[...]

    def relative_products(half, c):
        rows = pl.ds(pl.multiple_of(c * ROWS, ROWS), ROWS)
        wide_scr[rows, :] = dot(duns[half][rows, :], rc_scr[...])
        lanes = pl.ds(pl.multiple_of(c * part, part), part)
        four_scr[:, lanes] = dot_tn(qbs[half], duns[half][:, lanes])

    def first_head(c, carry):
        rows = pl.ds(pl.multiple_of(c * ROWS, ROWS), ROWS)
        unskew(ds_ref, dun0_scr, 0, c)
        for half in range(2):
            dqk_scr[half, rows, :] = dot(ds_ref[half, rows, :], k)
        return carry

    def second_head(c, carry):
        unskew(ds_ref, dun1_scr, 1, c)
        relative_products(0, c)
        return carry

    def finish(half):
        own = own_lanes(half)
        wide = wide_scr[...] * scale
        slot = lax.broadcasted_iota(jnp.int32, (frames, LANES), 1) // HEAD_DIM
        place = 3 - lax.broadcasted_iota(jnp.int32, (frames, LANES), 0) % 4
        picked = jnp.where(slot == place, wide[:, :LANES], 0.0)
        picked += jnp.where(slot + 2 == place, wide[:, LANES:], 0.0)
        dq_r = jnp.where(own, picked + pltpu.roll(picked, HEAD_DIM, 1), 0.0)
        dq_k = jnp.where(own, dqk_scr[half] * scale, 0.0)
        four = four_scr[...]
        dr_t = four[:HEAD_DIM]
        for s in (1, 2, 3):
            dr_t += pltpu.roll(four[s * HEAD_DIM : (s + 1) * HEAD_DIM], s, 1)
        return dq_k, dq_r, dr_t

    lax.fori_loop(0, frames // ROWS, first_head, 0)
    lax.fori_loop(0, frames // ROWS, second_head, 0)
    dq_k0, dq_r0, dr_t0 = finish(0)
    rc_scr[...] = four_rows(r_ref, r_scr, own_lanes(1))
    wide_scr[...] = dot(dun1_scr[...], rc_scr[...])
    four_scr[...] = dot_tn(qbs[1], dun1_scr[...])
    dq_k1, dq_r1, dr_t1 = finish(1)
    dq_k, dq_r = dq_k0 + dq_k1, dq_r0 + dq_r1
    dq_ref[...] = (dq_k + dq_r).astype(BF)
    du_ref[...] = jnp.sum(dq_k, axis=0, keepdims=True)
    db_ref[...] = jnp.sum(dq_r, axis=0, keepdims=True)
    dr_ref[...] = jnp.concatenate([dr_t0, dr_t1], axis=0).T.astype(BF)


def queries_back(q, k, rel, b, scores):
    frames, width = q.shape
    return pairs_call(
        queries_back_kernel,
        "queries_back",
        [(q, frames), (k, KEYS), (rel, RELS), (b, 1), (scores, 0)],
        [
            ((frames, width), BF, frames),
            ((RELS, width), BF, RELS),
            ((1, width), F32, 1),
            ((1, width), F32, 1),
        ],
        [
            ((frames, RELS), BF),
            ((frames, RELS), BF),
            ((RELS + 8, LANES), F32),
            ((RELS, 2 * LANES), BF),
            ((2, frames, LANES), F32),
            ((frames, 2 * LANES), F32),
            ((2 * LANES, RELS), F32),
        ],
        frames * LANES * (KEYS + 2 * RELS),
    )


MESH = pl.DeviceIdType.MESH


def grid_of(items, seq):
    side = math.isqrt(items)
    return side, seq // 2


def whereabouts(side):
    item, place = lax.axis_index("items"), lax.axis_index("seq")
    return item // side, item % side, place // 2, place % 2


def at_device(side, y, x, z, core):
    return (y * side + x, z * 2 + core)


def meet(partners):
    barrier = pltpu.get_barrier_semaphore()
    for partner in partners:
        pl.semaphore_signal(barrier, inc=1, device_id=partner, device_id_type=MESH)
    pl.semaphore_wait(barrier, len(partners))


def all_partners(side, depth, y, x, z, core):
    return (
        [at_device(side, y, x, z, 1 - core)]
        + [at_device(side, y, (x + d) % side, z, core) for d in range(1, side)]
        + [at_device(side, (y + d) % side, x, z, core) for d in range(1, side)]
        + [at_device(side, y, x, (z + d) % depth, core) for d in range(1, depth)]
    )


def send(source, target, send_sem, recv_sem, device):
    copy = pltpu.make_async_remote_copy(
        src_ref=source, dst_ref=target, send_sem=send_sem, recv_sem=recv_sem,
        device_id=device, device_id_type=MESH,
    )
    copy.start()
    return copy


AHEAD = 4
LAG = 2


def gather_order(p):
    if p % 8 == 4:
        return "yxz" if p % 16 == 4 else "xyz"
    return "zxy" if p % 2 else "zyx"


def gather_kernel(side, depth, pieces, count, *refs):
    shards, outs = refs[:count], refs[count : 2 * count]
    own_sem, s_sem, r_sem, cs_sem, cr_sem = refs[2 * count :]
    y, x, z, core = whereabouts(side)
    meet(all_partners(side, depth, y, x, z, core))
    owns = [
        pltpu.make_async_copy(shard, out.at[y, x, z, core], own_sem.at[i])
        for i, (shard, out) in enumerate(zip(shards, outs))
    ]
    for own in owns:
        own.start()
    copies = {}

    def region(p, done):
        i, cols = pieces[p]
        every = slice(None)
        return outs[i].at[
            every if "y" in done else y,
            every if "x" in done else x,
            every if "z" in done else z,
            core, :, cols,
        ]

    def start(p, k):
        order = gather_order(p)
        axis = order[k]
        here = region(p, order[:k])
        i, cols = pieces[p]
        copies[p, k] = [
            send(
                here if k else shards[i].at[:, cols], here,
                s_sem.at[k, p, d - 1], r_sem.at[k, p, d - 1],
                at_device(
                    side,
                    (y + d) % side if axis == "y" else y,
                    (x + d) % side if axis == "x" else x,
                    (z + d) % depth if axis == "z" else z,
                    core,
                ),
            )
            for d in range(1, depth if axis == "z" else side)
        ]

    def arrived(p, k):
        for copy in copies[p, k]:
            copy.wait_recv()

    for p in range(min(AHEAD, len(pieces))):
        start(p, 0)
    for own in owns:
        own.wait()
    for t in range(len(pieces) + 3 * LAG):
        if t + AHEAD < len(pieces):
            start(t + AHEAD, 0)
        for k in (1, 2):
            p = t - (k - 1) * LAG
            if 0 <= p < len(pieces):
                arrived(p, k - 1)
                start(p, k)
        p = t - 2 * LAG
        if 0 <= p < len(pieces):
            arrived(p, 2)
            here = region(p, "yxz")
            copies[p, 3] = [
                send(here, here, cs_sem.at[p], cr_sem.at[p], at_device(side, y, x, z, 1 - core))
            ]
        p = t - 3 * LAG
        if 0 <= p < len(pieces):
            arrived(p, 3)
    for started in copies.values():
        for copy in started:
            copy.wait_send()


def gather_by_kernel(shards, side, depth):
    pieces = [
        (i, pl.ds(c, min(512, shard.shape[1])))
        for i, shard in enumerate(shards)
        for c in range(0, shard.shape[1], 512)
    ]
    dma = pltpu.SemaphoreType.DMA
    n = len(pieces)
    outs = pl.pallas_call(
        functools.partial(gather_kernel, side, depth, pieces, len(shards)),
        in_specs=[pl.BlockSpec(memory_space=pl.ANY)] * len(shards),
        out_specs=[pl.BlockSpec(memory_space=pl.ANY)] * len(shards),
        out_shape=[
            jax.ShapeDtypeStruct((side, side, depth, 2, *shard.shape), shard.dtype)
            for shard in shards
        ],
        scratch_shapes=[dma((len(shards),))]
        + [dma((3, n, max(side, depth) - 1))] * 2
        + [dma((n,))] * 2,
        compiler_params=pltpu.CompilerParams(
            collective_id=1, has_side_effects=True, vmem_limit_bytes=48 * 1024 * 1024
        ),
        name="gather",
    )(*shards)
    return [out.reshape(-1, out.shape[-1]) for out in outs]


def put_block(out_ref, piece, total):
    rows = total.shape[0]
    lane = lax.broadcasted_iota(jnp.int32, (rows, LANES), 1)
    each = LANES // 4
    for tile in range(total.shape[1] // LANES):
        some = total[:, tile * LANES : (tile + 1) * LANES]
        for q in range(4):
            turn = (each * (piece - q)) % LANES
            moved = pltpu.roll(some, turn, 1) if turn else some
            at = slice((4 * tile + q) * LANES, (4 * tile + q + 1) * LANES)
            rest = out_ref[:, at] if piece else jnp.zeros_like(some)
            out_ref[:, at] = jnp.where(lane // each == piece, moved, rest)


Z_FIRST = (6, 12)


def added(parts):
    if len(parts) == 2:
        return parts[0] + parts[1]
    return sum(part.astype(F32) for part in parts).astype(BF)


def scatter_kernel(side, depth, pieces, count, *refs):
    ops, (small_out, four_out, in_out, out_out) = refs[:count], refs[count : count + 4]
    l_buf, r_buf, sum_buf, g_buf, c_buf, a_buf, b_buf, z_buf = refs[count + 4 : count + 12]
    e_buf, f_buf, h_buf = refs[count + 12 : count + 15]
    l_sem, r_sem, cs_sem, cr_sem, as_sem, ar_sem, bs_sem, br_sem, zs_sem, zr_sem = refs[count + 15 :]
    y, x, z, core = whereabouts(side)
    rows, wide = g_buf.shape[-2:]
    section = depth * 2 * rows
    last = len(pieces)
    meet(all_partners(side, depth, y, x, z, core))

    def cols(p):
        return pl.ds(0, pieces[p][5])

    def z_first(p):
        return Z_FIRST.index(p) if p in Z_FIRST else None

    most = l_buf.shape[1]
    chunks = []
    for p, (left, *_) in enumerate(pieces):
        deep = most if left is None else ops[left].shape[0]
        chunks += [(p, k, min(most, deep - k)) for k in range(0, deep, most)]

    def load(s):
        p, k, many = chunks[s]
        left, left_at, right, right_at, place, many_cols = pieces[p]
        slot = s % 2
        if left is None:
            copies = [
                pltpu.make_async_copy(
                    ops[right], g_buf.at[p % 2, :, :, :, :, :, cols(p)], r_sem.at[slot]
                )
            ]
        else:
            copies = [
                pltpu.make_async_copy(
                    ops[left].at[pl.ds(k, many), pl.ds(left_at, wide)],
                    l_buf.at[slot, pl.ds(0, many)], l_sem.at[slot],
                ),
                pltpu.make_async_copy(
                    ops[right].at[pl.ds(k, many), pl.ds(right_at, many_cols)],
                    r_buf.at[slot, pl.ds(0, many), cols(p)], r_sem.at[slot],
                ),
            ]
        for copy in copies:
            copy.start()
        return copies

    def multiply(s):
        p, k, many = chunks[s]
        slot = s % 2
        first, final = k == 0, k + many == ops[pieces[p][0]].shape[0]

        def section_product(i, carry):
            lanes = pl.ds(pl.multiple_of(i * section, section), section)
            total = dot_tn(l_buf[slot, 0:many, lanes], r_buf[slot, 0:many, cols(p)])
            if not first:
                total += sum_buf[lanes, cols(p)]
            if final:
                total = total.astype(BF).reshape(depth, 2, rows, pieces[p][5])
                g_buf[p % 2, i // side, i % side, :, :, :, cols(p)] = total
            else:
                sum_buf[lanes, cols(p)] = total
            return carry

        lax.fori_loop(0, side * side, section_product, 0)

    c_copies, a_copies, b_copies, z_copies = [], [], [], []
    loads = [load(0)]
    for t in range(last + 1 + 3 * LAG):
        p = t
        if p < last:
            if p >= 2:
                c_copies[p - 2].wait_send()
            for s in [s for s in range(len(chunks)) if chunks[s][0] == p]:
                if s + 1 < len(chunks):
                    loads.append(load(s + 1))
                for copy in loads[s]:
                    copy.wait()
                if pieces[p][0] is not None:
                    multiply(s)
            c_copies.append(
                send(
                    g_buf.at[p % 2, :, :, :, 1 - core, :, cols(p)],
                    c_buf.at[p, :, :, :, :, cols(p)],
                    cs_sem.at[p], cr_sem.at[p], at_device(side, y, x, z, 1 - core),
                )
            )
        p = t - 1
        if 0 <= p < last:
            c_copies[p].wait_recv()

            def add_core(i, carry, p=p):
                at = (i // side, i % side)
                c_buf[p, *at, :, :, cols(p)] += g_buf[p % 2, *at, :, core, :, cols(p)]
                return carry

            lax.fori_loop(0, side * side, add_core, 0)
            a_copies.append(
                [
                    send(
                        c_buf.at[p, :, :, (z + d) % depth, :, cols(p)],
                        e_buf.at[z_first(p), d - 1, :, :, :, cols(p)],
                        as_sem.at[p, d - 1], ar_sem.at[p, d - 1],
                        at_device(side, y, x, (z + d) % depth, core),
                    )
                    for d in range(1, depth)
                ]
                if z_first(p) is not None
                else [
                    send(
                        c_buf.at[p, (y + d) % side, :, :, :, cols(p)]
                        if p % 2
                        else c_buf.at[p, :, (x + d) % side, :, :, cols(p)],
                        a_buf.at[p, d - 1, :, :, :, cols(p)],
                        as_sem.at[p, d - 1], ar_sem.at[p, d - 1],
                        at_device(side, (y + d) % side, x, z, core)
                        if p % 2
                        else at_device(side, y, (x + d) % side, z, core),
                    )
                    for d in range(1, side)
                ]
            )
        p = t - 1 - LAG
        if 0 <= p < last:
            for copy in a_copies[p]:
                copy.wait_recv()

            def add_first(j, carry, p=p):
                own = c_buf[p, y, j, :, :, cols(p)] if p % 2 else c_buf[p, j, x, :, :, cols(p)]
                a_buf[p, 0, j, :, :, cols(p)] = added(
                    [own] + [a_buf[p, d, j, :, :, cols(p)] for d in range(side - 1)]
                )
                return carry

            q = z_first(p)
            if q is None:
                lax.fori_loop(0, side, add_first, 0)
            else:
                for j in range(side):
                    e_buf[q, 0, j, :, :, cols(p)] = added(
                        [c_buf[p, j, :, z, :, cols(p)]]
                        + [e_buf[q, d, j, :, :, cols(p)] for d in range(depth - 1)]
                    )
            b_copies.append(
                [
                    send(
                        e_buf.at[q, 0, :, (x + d) % side, :, cols(p)],
                        f_buf.at[q, d - 1, :, :, cols(p)],
                        bs_sem.at[p, d - 1], br_sem.at[p, d - 1],
                        at_device(side, y, (x + d) % side, z, core),
                    )
                    for d in range(1, side)
                ]
                if q is not None
                else [
                    send(
                        a_buf.at[p, 0, ((x if p % 2 else y) + d) % side, :, :, cols(p)],
                        b_buf.at[p, d - 1, :, :, cols(p)],
                        bs_sem.at[p, d - 1], br_sem.at[p, d - 1],
                        at_device(side, y, (x + d) % side, z, core)
                        if p % 2
                        else at_device(side, (y + d) % side, x, z, core),
                    )
                    for d in range(1, side)
                ]
            )
        p = t - 1 - 2 * LAG
        if 0 <= p < last:
            for copy in b_copies[p]:
                copy.wait_recv()

            q = z_first(p)
            if q is None:
                own = a_buf[p, 0, x if p % 2 else y, :, :, cols(p)]
                b_buf[p, 0, :, :, cols(p)] = added(
                    [own] + [b_buf[p, d, :, :, cols(p)] for d in range(side - 1)]
                )
            else:
                f_buf[q, 0, :, :, cols(p)] = added(
                    [e_buf[q, 0, :, x, :, cols(p)]]
                    + [f_buf[q, d, :, :, cols(p)] for d in range(side - 1)]
                )
            z_copies.append(
                [
                    send(
                        f_buf.at[q, 0, (y + d) % side, :, cols(p)],
                        h_buf.at[q, d - 1, :, cols(p)],
                        zs_sem.at[p, d - 1], zr_sem.at[p, d - 1],
                        at_device(side, (y + d) % side, x, z, core),
                    )
                    for d in range(1, side)
                ]
                if q is not None
                else [
                    send(
                        b_buf.at[p, 0, (z + d) % depth, :, cols(p)],
                        z_buf.at[p, d - 1, :, cols(p)],
                        zs_sem.at[p, d - 1], zr_sem.at[p, d - 1],
                        at_device(side, y, x, (z + d) % depth, core),
                    )
                    for d in range(1, depth)
                ]
            )
        p = t - 1 - 3 * LAG
        if 0 <= p < last:
            for copy in z_copies[p]:
                copy.wait_recv()
            q = z_first(p)
            total = (b_buf[p, 0, z, :, cols(p)] if q is None else f_buf[q, 0, y, :, cols(p)]).astype(F32)
            for d in range(depth - 1 if q is None else side - 1):
                total += (z_buf[p, d, :, cols(p)] if q is None else h_buf[q, d, :, cols(p)]).astype(F32)
            kind, index = pieces[p][4]
            if kind == 0:
                small_out[...] = total
            elif kind == 1:
                four_out[index] = total
            elif kind == 2:
                put_block(in_out, index, total)
            else:
                at = pieces[p][3]
                out_out[index * rows : (index + 1) * rows, at : at + pieces[p][5]] = total
    for p in range(last):
        for copy in ([c_copies[p]] if p >= last - 2 else []) + a_copies[p] + b_copies[p] + z_copies[p]:
            copy.wait_send()


def scatter_by_kernel(pairs, before, active, hidden, low, small, side, depth):
    width = low.shape[1]
    rows = width // (side * side * depth * 2)
    ops, pieces = [], []

    def operand(array):
        ops.append(array)
        return len(ops) - 1

    slabs = small.reshape(side, side, depth, 2, rows, small.shape[1])
    pieces.append((None, 0, operand(slabs), 0, (0, 0), small.shape[1]))
    seen, many = {}, 0
    for left, right in pairs:
        if id(left) not in seen:
            seen[id(left)] = operand(left)
        at_right = operand(right)
        for c in range(0, right.shape[1], width):
            pieces.append((seen[id(left)], 0, at_right, c, (1, many), width))
            many += 1
    at_hidden, at_before = operand(hidden), operand(before)
    at_active, at_low = operand(active), operand(low)
    steps = range(before.shape[1] // width)
    pieces += [(at_hidden, 0, at_before, c * width, (2, c), width) for c in steps]
    pieces += [(at_active, c * width, at_low, 0, (3, c), width) for c in steps]
    last = pieces.pop()
    pieces += [(*last[:3], at, last[4], width // 2) for at in (0, width // 2)]
    n = len(pieces)
    dma = pltpu.SemaphoreType.DMA
    outs = (
        (rows, small.shape[1]),
        (many, rows, width),
        (rows, before.shape[1]),
        (rows * len(steps), width),
    )
    return pl.pallas_call(
        functools.partial(scatter_kernel, side, depth, pieces, len(ops)),
        in_specs=[pl.BlockSpec(memory_space=pl.ANY)] * len(ops),
        out_specs=[pl.BlockSpec(memory_space=pltpu.VMEM)] * len(outs),
        out_shape=[jax.ShapeDtypeStruct(shape, F32) for shape in outs],
        scratch_shapes=[
            pltpu.VMEM((2, width, width), BF),
            pltpu.VMEM((2, width, width), BF),
            pltpu.VMEM((width, width), F32),
            pltpu.VMEM((2, side, side, depth, 2, rows, width), BF),
            pltpu.VMEM((n, side, side, depth, rows, width), BF),
            pltpu.VMEM((n, side - 1, side, depth, rows, width), BF),
            pltpu.VMEM((n, side - 1, depth, rows, width), BF),
            pltpu.VMEM((n, depth - 1, rows, width), BF),
            pltpu.VMEM((len(Z_FIRST), depth - 1, side, side, rows, width), BF),
            pltpu.VMEM((len(Z_FIRST), side - 1, side, rows, width), BF),
            pltpu.VMEM((len(Z_FIRST), side - 1, rows, width), BF),
            dma((2,)),
            dma((2,)),
            dma((n,)),
            dma((n,)),
        ]
        + [dma((n, max(side, depth) - 1))] * 6,
        compiler_params=pltpu.CompilerParams(
            collective_id=2, has_side_effects=True, vmem_limit_bytes=58 * 1024 * 1024
        ),
        name="scatter",
    )(*ops)


def products_kernel(ranges, *refs):
    p = pl.program_id(0)
    out_ref = refs[-1]
    section = 512
    for i, (first, count) in enumerate(ranges):
        left_ref, right_ref = refs[2 * i], refs[2 * i + 1]

        @pl.when((p >= first) & (p < first + count))
        def _(left_ref=left_ref, right_ref=right_ref):
            def part(j, carry):
                some = pl.ds(pl.multiple_of(j * section, section), section)
                out_ref[some, :] = dot_tn(left_ref[:, some], right_ref[...]).astype(BF)
                return carry

            lax.fori_loop(0, out_ref.shape[0] // section, part, 0)


def products(pairs):
    frames, width = pairs[0][0].shape
    specs, ops, ranges, first = [], [], [], 0
    for left, right in pairs:
        count = max(left.shape[1], right.shape[1]) // width
        for array in (left, right):
            most = array.shape[1] // width - 1
            specs.append(
                pl.BlockSpec(
                    (frames, width), lambda p, first=first, most=most: (0, jnp.clip(p - first, 0, most))
                )
            )
            ops.append(array)
        ranges.append((first, count))
        first += count
    return pl.pallas_call(
        functools.partial(products_kernel, ranges),
        grid=(first,),
        in_specs=specs,
        out_specs=pl.BlockSpec((width, width), lambda p: (0, p)),
        out_shape=jax.ShapeDtypeStruct((width, first * width), BF),
        compiler_params=pltpu.CompilerParams(vmem_limit_bytes=48 * 1024 * 1024),
        cost_estimate=pl.CostEstimate(
            flops=2 * frames * width * width * first,
            bytes_accessed=(3 * frames + 2 * width) * width * first,
            transcendentals=0,
        ),
        name="products",
    )(*ops)


def by_kernel(rows):
    items, seq = lax.axis_size("items"), lax.axis_size("seq")
    return rows % 16 == 0 and math.isqrt(items) ** 2 == items and items > 1 and seq > 2 and seq % 2 == 0


def norm(values):
    center = values - jnp.mean(values, axis=-1, keepdims=True)
    spread = jnp.mean(center * center, axis=-1, keepdims=True)
    scale = lax.rsqrt(spread + EPSILON)
    return center * scale, scale


def norm_back(grad, unit, scale, gain):
    inner = grad * gain
    mean_inner = jnp.mean(inner, axis=-1, keepdims=True)
    mean_both = jnp.mean(inner * unit, axis=-1, keepdims=True)
    return scale * (inner - mean_inner - unit * mean_both), jnp.sum(grad * unit, axis=0)


def silu_slope(value):
    s = jax.nn.sigmoid(value)
    return s * (1.0 + value * (1.0 - s))


def pack_in(shard, count):
    rows, hidden = shard.shape
    pieces = hidden // count // rows
    if 4 * rows == LANES and pieces == 4:
        return reorder(shard, True, shard.dtype)
    return shard.reshape(rows, count, pieces, rows).transpose(0, 2, 1, 3).reshape(rows, hidden)


def unpack_in(shard, count):
    rows, hidden = shard.shape
    pieces = hidden // count // rows
    if 4 * rows == LANES and pieces == 4:
        return reorder(shard, False, F32)
    return shard.reshape(rows, pieces, count, rows).transpose(0, 2, 1, 3).reshape(rows, hidden)


def pack_out(shard, rows):
    pieces, width = shard.shape[0] // rows, shard.shape[1]
    return shard.reshape(pieces, rows, width).transpose(1, 0, 2).reshape(rows, pieces * width)


def unpack_out(shard, width):
    rows, pieces = shard.shape[0], shard.shape[1] // width
    return shard.reshape(rows, pieces, width).transpose(1, 0, 2).reshape(rows * pieces, width)


def reorder_kernel(to_pieces, in_ref, out_ref):
    each = LANES // 4
    tiles = in_ref.shape[1] // LANES // 4
    lane = lax.broadcasted_iota(jnp.int32, (in_ref.shape[0], LANES), 1)

    def tile(at):
        return in_ref[:, at * LANES : (at + 1) * LANES].astype(F32)

    for k in range(tiles):
        for c in range(4):
            total = None
            for q in range(4):
                some = tile(4 * k + q) if to_pieces else tile(q * tiles + k)
                turn = each * (q - c) % LANES
                some = pltpu.roll(some, turn, 1) if turn else some
                total = some if total is None else jnp.where(lane // each == q, some, total)
            at = (c * tiles + k) if to_pieces else (4 * k + c)
            out_ref[:, at * LANES : (at + 1) * LANES] = total.astype(out_ref.dtype)


def reorder(shard, to_pieces, dtype):
    return pl.pallas_call(
        functools.partial(reorder_kernel, to_pieces),
        out_shape=jax.ShapeDtypeStruct(shard.shape, dtype),
        name="reorder",
    )(shard)


def halves(size):
    return [pl.ds(0, size // 2), pl.ds(size // 2, size // 2)]


def feed_forward_kernel(hid_ref, in_ref, out_w_ref, active_ref, slope_ref, out_ref):
    @pl.when(pl.program_id(0) == 0)
    def _():
        out_ref[...] = jnp.zeros_like(out_ref)

    parts = halves(in_ref.shape[1])
    befores = [dot(hid_ref[...], in_ref[:, at]) for at in parts]
    actives = []
    for at, before in zip(parts, befores):
        gate = jax.nn.sigmoid(before)
        active = (before * gate).astype(BF)
        active_ref[:, at] = active
        slope_ref[:, at] = (gate * (1.0 + before * (1.0 - gate))).astype(BF)
        actives.append(active)
    out_ref[...] += sum(dot(active, out_w_ref[at, :]) for at, active in zip(parts, actives))


def feed_forward_back_kernel(low_ref, in_ref, out_w_ref, slope_ref, before_ref, hid_ref):
    @pl.when(pl.program_id(0) == 0)
    def _():
        hid_ref[...] = jnp.zeros_like(hid_ref)

    parts = halves(in_ref.shape[1])
    actives = [dot_nt(low_ref[...], out_w_ref[at, :]) for at in parts]
    befores = []
    for at, active in zip(parts, actives):
        before = (active * slope_ref[:, at].astype(F32)).astype(BF)
        before_ref[:, at] = before
        befores.append(before)
    hid_ref[...] += sum(dot_nt(before, in_ref[:, at]) for at, before in zip(parts, befores))


def hidden_blocks(frames, width, hidden_width):
    step = width // 2
    per = width // step
    return (
        hidden_width // step,
        pl.BlockSpec((frames, width), lambda j: (0, 0)),
        pl.BlockSpec((width, step), lambda j: (0, j)),
        pl.BlockSpec((step, width), lambda j: (j % per, j // per)),
        pl.BlockSpec((frames, step), lambda j: (0, j)),
    )


def feed_forward(hidden, weight_in, weight_out):
    frames, width = hidden.shape
    hidden_width = weight_in.shape[1]
    steps, whole, in_block, out_block, unit_block = hidden_blocks(frames, width, hidden_width)
    units = jax.ShapeDtypeStruct((frames, hidden_width), BF)
    return pl.pallas_call(
        feed_forward_kernel,
        grid=(steps,),
        in_specs=[whole, in_block, out_block],
        out_specs=[unit_block, unit_block, whole],
        out_shape=[units, units, jax.ShapeDtypeStruct((frames, width), F32)],
        compiler_params=pltpu.CompilerParams(vmem_limit_bytes=48 * 1024 * 1024),
        cost_estimate=pl.CostEstimate(
            flops=4 * frames * width * hidden_width,
            bytes_accessed=4 * (width + frames) * hidden_width,
            transcendentals=frames * hidden_width,
        ),
        name="feed_forward",
    )(hidden, weight_in, weight_out)


def feed_forward_back(grad, slope, weight_in, weight_out):
    frames, width = grad.shape
    hidden_width = weight_in.shape[1]
    low = (0.5 * grad).astype(BF)
    steps, whole, in_block, out_block, unit_block = hidden_blocks(frames, width, hidden_width)
    before, hid = pl.pallas_call(
        feed_forward_back_kernel,
        grid=(steps,),
        in_specs=[whole, in_block, out_block, unit_block],
        out_specs=[unit_block, whole],
        out_shape=[
            jax.ShapeDtypeStruct((frames, hidden_width), BF),
            jax.ShapeDtypeStruct((frames, width), F32),
        ],
        compiler_params=pltpu.CompilerParams(vmem_limit_bytes=48 * 1024 * 1024),
        cost_estimate=pl.CostEstimate(
            flops=4 * frames * width * hidden_width,
            bytes_accessed=4 * (width + frames) * hidden_width,
            transcendentals=0,
        ),
        name="feed_forward_back",
    )(low, weight_in, weight_out, slope)
    return hid, before, low


def depthwise_kernel(wide_ref, taps_ref, out_ref):
    step = 64
    for first in range(0, out_ref.shape[0], step):
        total = jnp.zeros((step, LANES), F32)
        for k in range(TAPS):
            total += taps_ref[k : k + 1, :] * wide_ref[first + k : first + k + step, :]
        out_ref[first : first + step, :] = total


def depthwise(wide, taps):
    rows, width = wide.shape
    column = lambda rows: pl.BlockSpec((rows, LANES), lambda i: (0, i))
    return pl.pallas_call(
        depthwise_kernel,
        grid=(width // LANES,),
        in_specs=[column(rows), column(TAPS)],
        out_specs=column(rows - 2 * HALF),
        out_shape=jax.ShapeDtypeStruct((rows - 2 * HALF, width), F32),
        cost_estimate=pl.CostEstimate(
            flops=2 * rows * width * TAPS, bytes_accessed=8 * rows * width, transcendentals=0
        ),
        name="depthwise",
    )(wide, taps)


def depthwise_back_kernel(wide_ref, grad_ref, taps_ref, out_ref, dtaps_ref):
    step = 64
    frames = out_ref.shape[0]
    for first in range(0, frames, step):
        total = jnp.zeros((step, LANES), F32)
        for k in range(TAPS):
            at = first + 2 * HALF - k
            total += taps_ref[k : k + 1, :] * grad_ref[at : at + step, :]
        out_ref[first : first + step, :] = total
    sums = [jnp.zeros((8, LANES), F32)] * TAPS
    for first in range(0, frames, 8):
        grad = grad_ref[first + HALF : first + HALF + 8, :]
        sums = [sums[k] + grad * wide_ref[first + k : first + k + 8, :] for k in range(TAPS)]
    for k in range(TAPS):
        dtaps_ref[k : k + 1, :] = jnp.sum(sums[k], axis=0, keepdims=True)


def depthwise_back(wide, grad, taps):
    rows, width = wide.shape
    frames = rows - 2 * HALF
    column = lambda rows: pl.BlockSpec((rows, LANES), lambda i: (0, i))
    return pl.pallas_call(
        depthwise_back_kernel,
        grid=(width // LANES,),
        in_specs=[column(rows), column(rows), column(TAPS)],
        out_specs=[column(frames), column(TAPS)],
        out_shape=[
            jax.ShapeDtypeStruct((frames, width), F32),
            jax.ShapeDtypeStruct((TAPS, width), F32),
        ],
        cost_estimate=pl.CostEstimate(
            flops=4 * rows * width * TAPS, bytes_accessed=12 * rows * width, transcendentals=0
        ),
        name="depthwise_back",
    )(wide, grad, taps)


def shifted(values, by):
    size = lax.axis_size("seq")
    pairs = [(i, i + by) for i in range(size) if 0 <= i + by < size]
    return lax.ppermute(values, "seq", pairs)


def all_gather(shard):
    return lax.all_gather(shard, AXES, axis=0, tiled=True)


def gather_each(shards):
    if by_kernel(shards[0].shape[0]):
        side, depth = grid_of(lax.axis_size("items"), lax.axis_size("seq"))
        return gather_by_kernel(shards, side, depth)
    return [all_gather(shard) for shard in shards]


def scatter_sum(grads):
    return lax.psum_scatter(grads, AXES, scatter_dimension=0, tiled=True)


def scatter_each(pairs, before, active, hidden, low, small):
    count = lax.axis_size("items") * lax.axis_size("seq")
    width = low.shape[1]
    rows = width // count
    if by_kernel(rows):
        side, depth = grid_of(lax.axis_size("items"), lax.axis_size("seq"))
        return scatter_by_kernel(pairs, before, active, hidden, low, small, side, depth)
    steps = range(0, before.shape[1], width)
    columns = [small] + [dot_tn(left, right).astype(BF) for left, right in pairs]
    many = sum(right.shape[1] for left, right in pairs)
    columns.append(dot_tn(hidden, before).astype(BF))
    columns += [dot_tn(active[:, c : c + width], low).astype(BF) for c in steps]
    total = scatter_sum(jnp.concatenate(columns, axis=1)).astype(F32)
    small, total = total[:, : small.shape[1]], total[:, small.shape[1] :]
    return (
        small,
        [total[:, i : i + width] for i in range(0, many, width)],
        unpack_in(total[:, many : many + before.shape[1]], count),
        unpack_out(total[:, many + before.shape[1] :], width),
    )


def after(value, earlier):
    return value + jnp.minimum(jnp.abs(earlier[0, 0]), 0).astype(value.dtype)


def body(
    features, item_spans, item_lengths,
    ffn1_gain, ffn1_in, ffn1_out, att_gain, w_query, w_key, w_value, w_pos, u_bias, v_bias, w_out,
    conv_gain, conv_in, depth_kernel, inner_gain, conv_out, ffn2_gain, ffn2_in, ffn2_out, final_gain,
    cotangent,
):
    count = lax.axis_size("items") * lax.axis_size("seq")
    block = lax.axis_index("seq")
    frames, width = features.shape[1], features.shape[2]
    rows = w_query.shape[0]
    hidden_width = ffn1_in.shape[1]

    spans, lengths = item_spans[0], item_lengths[0]
    places = jnp.arange(spans.shape[0], dtype=jnp.int32)
    starts = lax.cummax(jnp.where(spans > 0, places, 0), axis=0)
    start = jnp.take(starts, block)
    live = jnp.take(lengths, start)
    place = block - start
    near_before = jnp.where((block > 0) & (jnp.take(starts, jnp.maximum(block - 1, 0)) == start), 1.0, 0.0)
    last = spans.shape[0] - 1
    near_after = jnp.where((block < last) & (jnp.take(starts, jnp.minimum(block + 1, last)) == start), 1.0, 0.0)
    live_mask = (place * BLOCK + jnp.arange(frames, dtype=jnp.int32) < live).astype(F32)[:, None]

    vectors = jnp.concatenate(
        [ffn1_gain, att_gain, u_bias, v_bias, conv_gain, inner_gain, ffn2_gain, final_gain]
    )
    small = jnp.concatenate([depth_kernel, vectors.reshape(8, rows)], axis=0)
    small = jnp.pad(small, ((0, SMALL - small.shape[0]), (0, 0))).T
    table, w1_in, w1_out, w_q, w_k, w_v, w_r = gather_each(
        [small, pack_in(ffn1_in, count), pack_out(ffn1_out, rows), w_query, w_key, w_value, w_pos]
    )
    set_two = all_gather(
        jnp.concatenate(
            [
                after(w_out, w_r), conv_in, conv_out,
                pack_in(ffn2_in, count), pack_out(ffn2_out, rows),
            ],
            axis=1,
        )
    )
    table = table.T.astype(F32)
    taps = table[:TAPS]
    g_ffn1, g_att, g_u, g_v, g_conv, g_inner, g_ffn2, g_final = (table[TAPS + i] for i in range(8))
    w_o = set_two[:, :width]
    c_in = set_two[:, width : 3 * width]
    c_out = set_two[:, 3 * width : 4 * width]
    w2_in = set_two[:, 4 * width : 4 * width + hidden_width]
    w2_out = set_two[:, 4 * width + hidden_width :]

    distance = (BLOCK - 1 + BLOCK * place - jnp.arange(RELS, dtype=jnp.int32)).astype(F32)
    frequency = 1.0 / 10000.0 ** (jnp.arange(0, width, 2).astype(F32) / width)
    angles = distance[:, None] * frequency[None, :]
    waves = jnp.concatenate([jnp.sin(angles), jnp.cos(angles)], axis=1).astype(BF)

    stream = features[0]
    unit1, scale1 = norm(stream)
    hid1 = (unit1 * g_ffn1).astype(BF)
    active1, slope1, out1 = feed_forward(hid1, w1_in, w1_out)
    first = stream + 0.5 * out1

    unit2, scale2 = norm(first)
    hid2 = (unit2 * g_att).astype(BF)
    nearby = [shifted(hid2, 2), shifted(hid2, 1), hid2, shifted(hid2, -1), shifted(hid2, -2)]
    queries = dot(hid2, w_q).astype(BF)
    relative = dot(waves, w_r).astype(BF)
    u_row, v_row = g_u[None].astype(BF), g_v[None].astype(BF)
    positional = relative_scores(queries, relative, v_row)
    key_hid = lax.dynamic_slice_in_dim(jnp.concatenate(nearby, axis=0), (2 - place) * BLOCK, KEYS, 0)
    keys = dot(key_hid, w_k).astype(BF)
    values = dot(key_hid, w_v).astype(BF)
    mixed, shares, inverses = attend(live.reshape(1), queries, keys, values, u_row, positional)
    second = first + dot(mixed, w_o)

    unit3, scale3 = norm(second)
    hid3 = (unit3 * g_conv).astype(BF)
    doubled = dot(hid3, c_in)
    linear, gate = doubled[:, :width], jax.nn.sigmoid(doubled[:, width:])
    glu = (linear * gate * live_mask).astype(BF)
    wide = jnp.concatenate(
        [
            shifted(glu[frames - HALF :], 1).astype(F32) * near_before,
            glu.astype(F32),
            shifted(glu[:HALF], -1).astype(F32) * near_after,
        ],
        axis=0,
    )
    depth = depthwise(wide, taps)
    unit4, scale4 = norm(depth)
    inner = unit4 * g_inner
    active4 = jax.nn.silu(inner).astype(BF)
    third = second + dot(active4, c_out)

    unit5, scale5 = norm(third)
    hid5 = (unit5 * g_ffn2).astype(BF)
    active5, slope5, out5 = feed_forward(hid5, w2_in, w2_out)
    fourth = third + 0.5 * out5
    unit6, scale6 = norm(fourth)
    layer_out = unit6 * g_final

    grad, d_final = norm_back(cotangent[0], unit6, scale6, g_final)
    d_hid5, d_before5, low5 = feed_forward_back(grad, slope5, w2_in, w2_out)
    d_third, d_ffn2 = norm_back(d_hid5, unit5, scale5, g_ffn2)
    grad = grad + d_third
    low4 = grad.astype(BF)
    packed, low4 = lax.optimization_barrier(
        (products([(hid5, d_before5), (active5, low5), (active4, low4)]), low4)
    )
    sum_one = scatter_sum(packed)

    d_active4 = dot_nt(low4, c_out)
    d_depth, d_inner = norm_back(d_active4 * silu_slope(inner), unit4, scale4, g_inner)
    d_depth = d_depth.astype(BF)
    d_wide = jnp.concatenate(
        [
            shifted(d_depth[frames - HALF :], 1).astype(F32) * near_before,
            d_depth.astype(F32),
            shifted(d_depth[:HALF], -1).astype(F32) * near_after,
        ],
        axis=0,
    )
    d_glu, d_taps = depthwise_back(wide, d_wide, taps)
    d_glu = d_glu * live_mask
    d_doubled = jnp.concatenate(
        [(d_glu * gate).astype(BF), (d_glu * linear * gate * (1.0 - gate)).astype(BF)], axis=1
    )
    d_second, d_conv = norm_back(dot_nt(d_doubled, c_in), unit3, scale3, g_conv)
    grad = grad + d_second

    low2 = grad.astype(BF)
    d_mixed = dot_nt(low2, w_o).astype(BF)
    d_scores, d_k, d_v = keys_back(queries, values, u_row, d_mixed, mixed, inverses, shares)
    d_near = dot_nt(d_k, w_k) + dot_nt(d_v, w_v)
    d_own = lax.dynamic_slice_in_dim(d_near, place * BLOCK, BLOCK, 0)
    d_all = lax.dynamic_update_slice_in_dim(
        jnp.zeros((5 * BLOCK, width), BF), d_near.astype(BF), (2 - place) * BLOCK, 0
    )
    returned = [
        shifted(d_all[(2 + by) * BLOCK : (3 + by) * BLOCK], by).astype(F32) for by in (-2, -1, 1, 2)
    ]
    d_q, d_r, d_u, d_b = queries_back(queries, keys, relative, v_row, d_scores)
    d_hid2 = dot_nt(d_q, w_q) + d_own + sum(returned)
    d_first, d_att = norm_back(d_hid2, unit2, scale2, g_att)
    grad = grad + d_first

    d_hid1, d_before1, low1 = feed_forward_back(grad, slope1, w1_in, w1_out)
    d_stream, d_ffn1 = norm_back(d_hid1, unit1, scale1, g_ffn1)
    input_grad = grad + d_stream

    vectors = jnp.stack([d_ffn1, d_att, d_u[0], d_b[0], d_conv, d_inner, d_ffn2, d_final], axis=0)
    small = jnp.concatenate([d_taps, vectors], axis=0)
    small = jnp.pad(small, ((0, SMALL - small.shape[0]), (0, 0))).T.astype(BF)
    small, input_grad = lax.optimization_barrier((small, input_grad))
    g_small, many, g1_in, g1_out = scatter_each(
        [
            (mixed, low2), (hid3, d_doubled),
            (hid2, d_q), (key_hid, d_k), (key_hid, d_v), (waves, d_r),
        ],
        d_before1, active1, hid1, low1, small,
    )

    sum_one = sum_one.astype(F32)
    w = width
    h = hidden_width
    gains = [g_small[:, TAPS + i] for i in range(8)]
    return (
        layer_out[None],
        input_grad[None],
        gains[0],
        g1_in,
        g1_out,
        gains[1],
        many[3],
        many[4],
        many[5],
        many[6],
        gains[2],
        gains[3],
        many[0],
        gains[4],
        jnp.concatenate([many[1], many[2]], axis=1),
        g_small[:, :TAPS].T,
        gains[5],
        sum_one[:, 2 * h :],
        gains[6],
        unpack_in(sum_one[:, :h], count),
        unpack_out(sum_one[:, h : 2 * h], w),
        gains[7],
    )


def solution(mesh):
    both = ("items", "seq")
    lead = P("items", "seq", None)
    group = P("items", None)
    flat = P(both)
    tall = P(both, None)
    side = P(None, both)
    return jax.shard_map(
        body,
        mesh=mesh,
        in_specs=(
            lead, group, group,
            flat, tall, tall, flat, tall, tall, tall, tall, flat, flat, tall,
            flat, tall, side, flat, tall, flat, tall, tall, flat,
            lead,
        ),
        out_specs=(
            lead, lead,
            flat, tall, tall, flat, tall, tall, tall, tall, flat, flat, tall,
            flat, tall, side, flat, tall, flat, tall, tall, flat,
        ),
        check_vma=False,
    )
```

time: 4970 us -> 827 us (0.17)
  local copies, waits for them, and re-layouts: 1840 us -> 62.5 us
  waiting for transfers between devices: 1430 us -> 3.03 us
  matrix products: 863 us -> 58.6 us
  Pallas kernels: 0 us -> 583 us
  blocking collectives: 253 us -> 0 us
  other arithmetic: 308 us -> 57.2 us
  loops' own time: 190 us -> 0 us
    reduce_scatter x11 -> x1, waiting for transfers between devices: 1210 us -> 0.01 us  [scatter_sum(): return lax.psum_scatter(grads, AXES, scatter_dimension=0, tiled=True)]
    dot_general x464 -> x13, matrix products: 863 us -> 58.6 us  [the longest x6 30.7 us: dot_nt(): lax.dot_general(left, right, (((1,), (1,)), ((), ())), preferred_element_...]
    reshape x196 -> x5, local copies, waits for them, and re-layouts: 596 us -> 1.97 us  [the longest x2 1.44 us: pack_out(): shard.reshape(pieces, rows, width).transpose(1, 0, 2)]
    pallas_call x0 -> x16, Pallas kernels: none -> 583 us  [the longest x1 169 us: scatter_by_kernel(): pl.pallas_call(functools.partial(scatter_kernel, side, depth, pieces, len...]
    dynamic_slice x218 -> x1, local copies, waits for them, and re-layouts: 255 us -> 0.31 us  [body(): lax.dynamic_slice_in_dim(jnp.concatenate(nearby, axis=0), (2 - place) * B...]
    pad x96 -> x0, local copies, waits for them, and re-layouts: 221 us -> none  [the longest x48 144 us: relative_shift(): lax.slice(flattened, (BLOCK - 1,), (BLOCK - 1 + BLOCK * (2 * BLOCK - 1),))]
    while x1368 -> x0, local copies, waits for them, and re-layouts: 197 us -> none
    all_gather x11 -> x1, waiting for transfers between devices: 191 us -> 0.01 us  [all_gather(): return lax.all_gather(shard, AXES, axis=0, tiled=True)]
  transfers between devices with their start and end apart: 32 -> 14, of which waited for: 14 -> 1; matrix products, arithmetic and copies ran while one was open for 57% -> 14% of each run, Pallas kernels for 0% -> 49%
where the time goes in v1:
time: 827 us; the launch traced here: 818 us
  Pallas kernels  583 us (70%)
  local copies, waits for them, and re-layouts  62.5 us (8%)
  matrix products  58.6 us (7%)
  other arithmetic  57.2 us (7%)
  starting transfers between devices  34.5 us (4%)
  between operations  18.9 us (2%)
    pallas_call x1, Pallas kernels, scatter_by_kernel(): pl.pallas_call(functools.partial(scatter_kernel, side, depth, pieces, len...  169 us
    pallas_call x1, Pallas kernels, gather_by_kernel(): pl.pallas_call(functools.partial(gather_kernel, side, depth, pieces, len(...  123 us
    pallas_call x2, Pallas kernels, heads_call(): pl.pallas_call(kernel, grid=(pairs, 2), in_specs=[spec for _, spec in ins...  104 us
    pallas_call x2, Pallas kernels, pairs_call(): pl.pallas_call(kernel, grid=(pairs,), in_specs=[spec(a.shape, rows) for a...  85.9 us
    ppermute x12, starting transfers between devices, shifted(): return lax.ppermute(values, 'seq', pairs)  34.4 us
    unnamed x150, local copies, waits for them, and re-layouts  30.8 us
    dot_general x6, matrix products, dot_nt(): lax.dot_general(left, right, (((1,), (1,)), ((), ())), preferred_element_...  30.7 us
    pallas_call x2, Pallas kernels, feed_forward(): pl.pallas_call(feed_forward_kernel, grid=(steps,), in_specs=[whole, in_bl...  29.6 us
  transfers between devices with their start and end apart: 14, of which 1 were waited for; matrix products, arithmetic and copies ran while one was open for 14% of the time, Pallas kernels for 49%

profile of v1, /device:TPU:0, one launch (start us, length us, event | category | flops | bytes accessed | tf_op | source)
XLA Modules:
  0.0 818.1 jit_solution(5951426447815885746)
XLA Ops:
  10.6 5.4 concatenate.32
  21.3 122.6 %gather.18 = (bf16[2,2,4,2,32,128]{5,4,3,2,1,0:T(8,128)(2,1)S(1)}, bf16[2,2,4,2,32,4096]{5,4,3,2,1,0:T(8,128)(2,1)}, bf16[2,2,4,2,32,4096]{5,4,3,2,1,0:T(8,128)(...) custom-call(bf16[32,128]{1,0:T(8,128)(2,1)S(1)} %fusion.34.refs_0_, ...), custom_call_target="tpu_custom_call" | custom-call | tf_op jit(solution)/shard_map/gather/pallas_call | solution.py:552
  155.9 15.2 %feed_forward.2 = (bf16[512,4096]{1,0:T(8,128)(2,1)}, bf16[512,4096]{1,0:T(8,128)(2,1)}, f32[512,1024]{1,0:T(8,128)S(1)}) custom-call(bf16[512,1024]{1,0:T(8,128)(2,1)S(1)} %multiply_convert_fusion.10.hid_ref.refs_12_, bf16[1024,4096]{1,0:T(8,128)(2,1)} %bitcast.144, bf16[1024,4096]{1,0:T(8,128)(2,1)} %bitcast.146), custom_call_target="tpu_custom_call" | custom-call | flops 8589934592 | bytes 25165824 | tf_op jit(solution)/shard_map/feed_forward/pallas_call | solution.py:1064
  172.7 6.3 collective-permute-start
  187.8 15.8 %fusion = (bf16[2048,512]{1,0:T(8,128)(2,1)S(1)}, bf16[2048,512]{1,0:T(8,128)(2,1)S(1)}) fusion(f32[512]{0:T(512)S(1)} %negate_power_fusion, f32[2048]{0:T(1024)S(1)} %subtract_convert_fusion), kind=kLoop, calls=%fused_computation.3 | loop fusion | flops 3145728 | bytes 4204544 | tf_op jit(solution)/shard_map/convert.20
  208.4 50.4 %positions.1.pos_ref = f32[16,512,1536]{2,1,0:T(8,128)} custom-call(bf16[512,1024]{1,0:T(8,128)(2,1)S(1)} %convolution_convert_fusion.3.q_ref, bf16[2048,1024]{1,0:T(8,128)(2,1)S(1)} %convolution_convert_fusion.2.r_ref, bf16[1,1024]{1,0:T(2,128)(2,1)S(1)} %get-tuple-element.254.b_ref), custom_call_target="tpu_custom_call" | custom-call | flops 17179869184 | bytes 55576576 | tf_op jit(solution)/shard_map/positions/pallas_call | solution.py:163
  274.0 4.8 convolution_convert_fusion.v_ref
  283.6 53.7 %attend.1 = (bf16[512,1024]{1,0:T(8,128)(2,1)S(1)}, bf16[16,512,1536]{2,1,0:T(8,128)(2,1)}, f32[512,1024]{1,0:T(8,128)S(1)}) custom-call(s32[1]{0:T(128)} %select_n.63.live_ref, bf16[512,1024]{1,0:T(8,128)(2,1)S(1)} %copy-done.18, bf16[1536,1024]{1,0:T(8,128)(2,1)} %convolution_convert_fusion.1.k_ref, bf16[1536,1024]{1,0:T(8,128)(2,1)} %convolution_convert_fusion.v_ref, ...), custom_call_target="tpu_custom_call" | custom-call | flops 25769803776 | bytes 85985280 | tf_op jit(solution)/shard_map/attend/pallas_call | solution.py:163
  345.2 5.3 fusion.4
  357.5 6.2 fusion.42
  365.5 7.6 depthwise.1
  381.0 14.4 %feed_forward.3 = (bf16[512,4096]{1,0:T(8,128)(2,1)}, bf16[512,4096]{1,0:T(8,128)(2,1)}, f32[512,1024]{1,0:T(8,128)S(1)}) custom-call(bf16[512,1024]{1,0:T(8,128)(2,1)S(1)} %multiply_convert_fusion.5.hid_ref.refs_0_, bf16[1024,4096]{1,0:T(8,128)(2,1)} %get-tuple-element.227.in_ref, bf16[1024,4096]{1,0:T(8,128)(2,1)} %get-tuple-element.226.out_w_ref), custom_call_target="tpu_custom_call" | custom-call | flops 8589934592 | bytes 25165824 | tf_op jit(solution)/shard_map/feed_forward/pallas_call | solution.py:1064
  400.3 14.2 %feed_forward_back.2 = (bf16[512,4096]{1,0:T(8,128)(2,1)}, f32[512,1024]{1,0:T(8,128)S(1)}) custom-call(bf16[512,1024]{1,0:T(8,128)(2,1)S(1)} %get-tuple-element.218.low_ref.refs_3_, bf16[1024,4096]{1,0:T(8,128)(2,1)} %get-tuple-element.227.in_ref, bf16[1024,4096]{1,0:T(8,128)(2,1)} %get-tuple-element.226.out_w_ref, ...), custom_call_target="tpu_custom_call" | custom-call | flops 8589934592 | bytes 25165824 | tf_op jit(solution)/shard_map/feed_forward_back/pallas_call | solution.py:1085
  417.6 18.4 %products.1 = bf16[1024,9216]{1,0:T(8,128)(2,1)} custom-call(bf16[512,1024]{1,0:T(8,128)(2,1)S(1)} %multiply_convert_fusion.5.hid_ref.refs_0_, bf16[512,4096]{1,0:T(8,128)(2,1)} %get-tuple-element.70.refs_1_, bf16[512,4096]{1,0:T(8,128)(2,1)} %get-tuple-element.71.refs_2_, bf16[512,1024]{1,0:T(8,128)(2,1)S(1)} %get-tuple-element.218.low_ref.refs_3_, ...), custom_call_target="tpu_custom_call" | custom-call | flops 9663676416 | bytes 33030144 | tf_op jit(solution)/shard_map/products/pallas_call | solution.py:917
  454.9 11.2 %depthwise_back.1 = (f32[512,1024]{1,0:T(8,128)}, f32[31,1024]{1,0:T(8,128)}) custom-call(f32[542,1024]{1,0:T(8,128)} %pad_maximum_fusion.1.wide_ref, f32[542,1024]{1,0:T(8,128)} %pad_maximum_fusion.2.grad_ref, f32[31,1024]{1,0:T(8,128)} %slice.210.taps_ref), custom_call_target="tpu_custom_call" | custom-call | flops 68820992 | bytes 6660096 | tf_op jit(solution)/shard_map/depthwise_back/pallas_call | solution.py:1151
  470.5 5.6 multiply_reduce_fusion.3
  481.3 29.4 %keys_back.1 = (bf16[16,512,1536]{2,1,0:T(8,128)(2,1)}, bf16[1536,1024]{1,0:T(8,128)(2,1)}, bf16[1536,1024]{1,0:T(8,128)(2,1)}) custom-call(bf16[512,1024]{1,0:T(8,128)(2,1)} %copy-done.17, bf16[1536,1024]{1,0:T(8,128)(2,1)} %convolution_convert_fusion.v_ref, bf16[1,1024]{1,0:T(2,128)(2,1)} %copy-done.11, bf16[512,1024]{1,0:T(8,128)(2,1)} %fusion.26.g_ref, ...), custom_call_target="tpu_custom_call" | custom-call | flops 38654705664 | bytes 65013760 | tf_op jit(solution)/shard_map/keys_back/pallas_call | solution.py:262
  510.7 5.5 fusion.51
  518.8 5.7 convert_dynamic-update-slice_fusion
  525.9 5.5 collective-permute-start.10
  537.7 56.5 %queries_back.1 = (bf16[512,1024]{1,0:T(8,128)(2,1)}, bf16[2048,1024]{1,0:T(8,128)(2,1)}, f32[1,1024]{1,0:T(1,128)}, f32[1,1024]{1,0:T(1,128)}) custom-call(bf16[512,1024]{1,0:T(8,128)(2,1)} %copy-done.17, bf16[1536,1024]{1,0:T(8,128)(2,1)} %convolution_convert_fusion.1.k_ref, bf16[2048,1024]{1,0:T(8,128)(2,1)} %copy-done.19, bf16[1,1024]{1,0:T(2,128)(2,1)} %copy-done.10, ...), custom_call_target="tpu_custom_call" | custom-call | flops 47244640256 | bytes 38807552 | tf_op jit(solution)/shard_map/queries_back/pallas_call | solution.py:262
  598.6 5.7 multiply_reduce_fusion.4
  606.5 14.8 %feed_forward_back.3 = (bf16[512,4096]{1,0:T(8,128)(2,1)}, f32[512,1024]{1,0:T(8,128)S(1)}) custom-call(bf16[512,1024]{1,0:T(8,128)(2,1)S(1)} %get-tuple-element.210.low_ref.refs_15_, bf16[1024,4096]{1,0:T(8,128)(2,1)} %bitcast.145, bf16[1024,4096]{1,0:T(8,128)(2,1)} %bitcast.147, bf16[512,4096]{1,0:T(8,128)(2,1)} %get-tuple-element.82.slope_ref), custom_call_target="tpu_custom_call" | custom-call | flops 8589934592 | bytes 25165824 | tf_op jit(solution)/shard_map/feed_forward_back/pallas_call | solution.py:1085
  627.4 168.8 %scatter.1 = (f32[32,128]{1,0:T(8,128)}, f32[7,32,1024]{2,1,0:T(8,128)}, f32[32,4096]{1,0:T(8,128)}, f32[128,1024]{1,0:T(8,128)}) custom-call(bf16[2,2,4,2,32,128]{5,4,3,2,1,0:T(8,128)(2,1)} %bitcast.119, bf16[512,1024]{1,0:T(8,128)(2,1)} %copy-done.4, bf16[512,1024]{1,0:T(8,128)(2,1)} %copy-done.42, bf16[512,1024]{1,0:T(8,128)(2,1)} %copy-done.41, ...), custom_call_target="tpu_custom_call" | custom-call | tf_op jit(solution)/shard_map/scatter/pallas_call | solution.py:855
  (292 shorter events, 150.3 us)
Async XLA Ops:
  7.2 256.1 %copy-start = (s32[1,8]{1,0:T(1,128)S(1)}, s32[1,8]{1,0:T(1,128)}, u32[]{:S(2)}) copy-start(s32[1,8]{1,0:T(1,128)} %param.26) | copy-start | bytes 100
  7.2 141.8 %copy-start.48 = (bf16[128,1024]{1,0:T(8,128)(2,1)S(1)}, bf16[128,1024]{1,0:T(8,128)(2,1)}, u32[]{:S(2)}) copy-start(bf16[128,1024]{1,0:T(8,128)(2,1)} %param.45) | copy-start | bytes 786436
  7.2 142.1 %copy-start.55 = (bf16[32,1024]{1,0:T(8,128)(2,1)S(1)}, bf16[32,1024]{1,0:T(8,128)(2,1)}, u32[]{:S(2)}) copy-start(bf16[32,1024]{1,0:T(8,128)(2,1)} %param.37) | copy-start | bytes 196612
  7.2 142.2 %copy-start.50 = (bf16[32,2048]{1,0:T(8,128)(2,1)S(1)}, bf16[32,2048]{1,0:T(8,128)(2,1)}, u32[]{:S(2)}) copy-start(bf16[32,2048]{1,0:T(8,128)(2,1)} %param.39) | copy-start | bytes 393220
  7.2 331.4 %all-gather.2.cloned.1.call-start = ((), (), s32[]{:S(2)}) async-start(), calls=%async_computation.1 | async-start | bytes 25952256 | tf_op jit(solution)/shard_map/all_gather | solution.py:1174
  7.3 142.1 %copy-start.56 = (bf16[32,1024]{1,0:T(8,128)(2,1)S(1)}, bf16[32,1024]{1,0:T(8,128)(2,1)}, u32[]{:S(2)}) copy-start(bf16[32,1024]{1,0:T(8,128)(2,1)} %param.42) | copy-start | bytes 196612
  151.3 651.0 %reduce-scatter.2.cloned.1.call-start = ((), (), s32[]{:S(2)}) async-start(), calls=%async_computation.2 | async-start | bytes 19464192 | tf_op jit(solution)/shard_map/reduce_scatter | solution.py:1185
  155.5 113.1 %copy-start.51 = (f32[1,1024]{1,0:T(1,128)}, f32[1,1024]{1,0:T(1,128)S(1)}, u32[]{:S(2)}) copy-start(f32[1,1024]{1,0:T(1,128)S(1)} %get-tuple-element.252) | copy-start | bytes 12292
  171.4 97.3 %copy-start.59 = (f32[512]{0:T(512)}, f32[512]{0:T(512)S(1)}, u32[]{:S(2)}) copy-start(f32[512]{0:T(512)S(1)} %broadcast_multiply_fusion.16) | copy-start | bytes 6148
  171.8 96.9 %copy-start.63 = (f32[512]{0:T(512)}, f32[512]{0:T(512)S(1)}, u32[]{:S(2)}) copy-start(f32[512]{0:T(512)S(1)} %add_rsqrt_fusion.4) | copy-start | bytes 6148
  172.7 93.1 %collective-permute-start = (bf16[512,1024]{1,0:T(8,128)(2,1)S(1)}, bf16[512,1024]{1,0:T(8,128)(2,1)}, u32[]{:S(2)}, u32[]{:S(2)}) collective-permute-start(bf16[512,1024]{1,0:T(8,128)(2,1)S(1)} %multiply_convert_fusion.9.refs_5_), channel_id=1, source_target_pairs={{0,2},{1,3},{2,4},{3,5},{4,6},{5,7},{8,10},{9,11},{10,12},{11,13},... | collective-permute-start | bytes 3145736 | tf_op jit(solution)/shard_map/ppermute | solution.py:1170
  179.0 88.3 %collective-permute-start.1 = (bf16[512,1024]{1,0:T(8,128)(2,1)S(1)}, bf16[512,1024]{1,0:T(8,128)(2,1)}, u32[]{:S(2)}, u32[]{:S(2)}) collective-permute-start(bf16[512,1024]{1,0:T(8,128)(2,1)S(1)} %multiply_convert_fusion.9.refs_5_), channel_id=1, source_target_pairs={{0,1},{1,2},{2,3},{3,4},{4,5},{5,6},{6,7},{8,9},{9,10},{10,11},{11... | collective-permute-start | bytes 3145736 | tf_op jit(solution)/shard_map/ppermute | solution.py:1170
  182.2 86.9 %collective-permute-start.2 = (bf16[512,1024]{1,0:T(8,128)(2,1)S(1)}, bf16[512,1024]{1,0:T(8,128)(2,1)}, u32[]{:S(2)}, u32[]{:S(2)}) collective-permute-start(bf16[512,1024]{1,0:T(8,128)(2,1)S(1)} %multiply_convert_fusion.9.refs_5_), channel_id=1, source_target_pairs={{1,0},{2,1},{3,2},{4,3},{5,4},{6,5},{7,6},{9,8},{10,9},{11,10},{12... | collective-permute-start | bytes 3145736 | tf_op jit(solution)/shard_map/ppermute | solution.py:1170
  183.5 86.9 %collective-permute-start.3 = (bf16[512,1024]{1,0:T(8,128)(2,1)S(1)}, bf16[512,1024]{1,0:T(8,128)(2,1)}, u32[]{:S(2)}, u32[]{:S(2)}) collective-permute-start(bf16[512,1024]{1,0:T(8,128)(2,1)S(1)} %multiply_convert_fusion.9.refs_5_), channel_id=1, source_target_pairs={{2,0},{3,1},{4,2},{5,3},{6,4},{7,5},{10,8},{11,9},{12,10},{13,11},... | collective-permute-start | bytes 3145736 | tf_op jit(solution)/shard_map/ppermute | solution.py:1170
  186.5 97.2 %copy-start.11 = (bf16[1,1024]{1,0:T(2,128)(2,1)}, bf16[1,1024]{1,0:T(2,128)(2,1)S(1)}, u32[]{:S(2)}) copy-start(bf16[1,1024]{1,0:T(2,128)(2,1)S(1)} %get-tuple-element.255.u_ref) | copy-start | bytes 6148
  352.7 11.1 %collective-permute-start.4 = (bf16[15,1024]{1,0:T(8,128)(2,1)S(1)}, bf16[15,1024]{1,0:T(8,128)(2,1)S(1)}, u32[]{:S(2)}, u32[]{:S(2)}) collective-permute-start(bf16[15,1024]{1,0:T(8,128)(2,1)S(1)} %get-tuple-element.237), channel_id=1, source_target_pairs={{0,1},{1,2},{2,3},{3,4},{4,5},{5,6},{6,7},{8,9},{9,10},{10,11},{11... | collective-permute-start | bytes 92168 | tf_op jit(solution)/shard_map/ppermute | solution.py:1170
  356.2 7.6 collective-permute-start.5
  442.0 8.3 %collective-permute-start.6 = (bf16[15,1024]{1,0:T(8,128)(2,1)S(1)}, bf16[15,1024]{1,0:T(8,128)(2,1)S(1)}, u32[]{:S(2)}, u32[]{:S(2)}) collective-permute-start(bf16[15,1024]{1,0:T(8,128)(2,1)S(1)} %get-tuple-element.235), channel_id=1, source_target_pairs={{0,1},{1,2},{2,3},{3,4},{4,5},{5,6},{6,7},{8,9},{9,10},{10,11},{11... | collective-permute-start | bytes 92168 | tf_op jit(solution)/shard_map/ppermute | solution.py:1170
  449.0 4.3 collective-permute-start.7
  525.9 71.3 %collective-permute-start.10 = (bf16[512,1024]{1,0:T(8,128)(2,1)}, bf16[512,1024]{1,0:T(8,128)(2,1)}, u32[]{:S(2)}, u32[]{:S(2)}) collective-permute-start(bf16[512,1024]{1,0:T(8,128)(2,1)} %get-tuple-element.232), channel_id=1, source_target_pairs={{0,1},{1,2},{2,3},{3,4},{4,5},{5,6},{6,7},{8,9},{9,10},{10,11},{11... | collective-permute-start | bytes 3145736 | tf_op jit(solution)/shard_map/ppermute | solution.py:1170
  531.4 65.9 %collective-permute-start.11 = (bf16[512,1024]{1,0:T(8,128)(2,1)S(1)}, bf16[512,1024]{1,0:T(8,128)(2,1)}, u32[]{:S(2)}, u32[]{:S(2)}) collective-permute-start(bf16[512,1024]{1,0:T(8,128)(2,1)S(1)} %get-tuple-element.231), channel_id=1, source_target_pairs={{0,2},{1,3},{2,4},{3,5},{4,6},{5,7},{8,10},{9,11},{10,12},{11,13},... | collective-permute-start | bytes 3145736 | tf_op jit(solution)/shard_map/ppermute | solution.py:1170
  535.1 62.2 %collective-permute-start.8 = (bf16[512,1024]{1,0:T(8,128)(2,1)S(1)}, bf16[512,1024]{1,0:T(8,128)(2,1)}, u32[]{:S(2)}, u32[]{:S(2)}) collective-permute-start(bf16[512,1024]{1,0:T(8,128)(2,1)S(1)} %get-tuple-element.230), channel_id=1, source_target_pairs={{2,0},{3,1},{4,2},{5,3},{6,4},{7,5},{10,8},{11,9},{12,10},{13,11},... | collective-permute-start | bytes 3145736 | tf_op jit(solution)/shard_map/ppermute | solution.py:1170
  536.4 60.9 %collective-permute-start.9 = (bf16[512,1024]{1,0:T(8,128)(2,1)S(1)}, bf16[512,1024]{1,0:T(8,128)(2,1)}, u32[]{:S(2)}, u32[]{:S(2)}) collective-permute-start(bf16[512,1024]{1,0:T(8,128)(2,1)S(1)} %get-tuple-element.233), channel_id=1, source_target_pairs={{1,0},{2,1},{3,2},{4,3},{5,4},{6,5},{7,6},{9,8},{10,9},{11,10},{12... | collective-permute-start | bytes 3145736 | tf_op jit(solution)/shard_map/ppermute | solution.py:1170
  537.7 59.6 %copy-start.52 = (f32[1,1024]{1,0:T(1,128)S(1)}, f32[1,1024]{1,0:T(1,128)}, u32[]{:S(2)}) copy-start(f32[1,1024]{1,0:T(1,128)} %copy-done.51) | copy-start | bytes 12292
  (59 other events, 556.8 us)
Sparse Core Ops, SparseCore 0:
  151.5 183.1 all-gather.1
  436.2 230.3 reduce-scatter.1

commit v2 on v1

--- a/solution.py
+++ b/solution.py
@@ -457,8 +457,8 @@
     return copy
 
 
-AHEAD = 4
-LAG = 2
+AHEAD = 6
+LAG = 3
 
 
 def gather_order(p):
@@ -1234,10 +1234,12 @@
     near_after = jnp.where((block < last) & (jnp.take(starts, jnp.minimum(block + 1, last)) == start), 1.0, 0.0)
     live_mask = (place * BLOCK + jnp.arange(frames, dtype=jnp.int32) < live).astype(F32)[:, None]
 
-    vectors = jnp.concatenate(
-        [ffn1_gain, att_gain, u_bias, v_bias, conv_gain, inner_gain, ffn2_gain, final_gain]
-    )
-    small = jnp.concatenate([depth_kernel, vectors.reshape(8, rows)], axis=0)
+    singles = [ffn1_gain, att_gain, u_bias, v_bias, conv_gain, inner_gain, ffn2_gain, final_gain]
+    order = lax.broadcasted_iota(jnp.int32, (len(singles), rows), 0)
+    vectors = jnp.broadcast_to(singles[0][None], order.shape)
+    for i, single in enumerate(singles):
+        vectors = jnp.where(order == i, single[None], vectors)
+    small = jnp.concatenate([depth_kernel, vectors], axis=0)
     small = jnp.pad(small, ((0, SMALL - small.shape[0]), (0, 0))).T
     table, w1_in, w1_out, w_q, w_k, w_v, w_r = gather_each(
         [small, pack_in(ffn1_in, count), pack_out(ffn1_out, rows), w_query, w_key, w_value, w_pos]

time: 827 us -> 819 us (level)
  no operation moved by 1% of the time
where the time goes in v2:
time: 819 us; the launch traced here: 810 us
  Pallas kernels  578 us (71%)
  matrix products  58.2 us (7%)
  other arithmetic  58.1 us (7%)
  local copies, waits for them, and re-layouts  56.3 us (7%)
  starting transfers between devices  36.3 us (4%)
  between operations  18.9 us (2%)
    pallas_call x1, Pallas kernels, scatter_by_kernel(): pl.pallas_call(functools.partial(scatter_kernel, side, depth, pieces, len...  165 us
    pallas_call x1, Pallas kernels, gather_by_kernel(): pl.pallas_call(functools.partial(gather_kernel, side, depth, pieces, len(...  121 us
    pallas_call x2, Pallas kernels, heads_call(): pl.pallas_call(kernel, grid=(pairs, 2), in_specs=[spec for _, spec in ins...  104 us
    pallas_call x2, Pallas kernels, pairs_call(): pl.pallas_call(kernel, grid=(pairs,), in_specs=[spec(a.shape, rows) for a...  87.4 us
    ppermute x12, starting transfers between devices, shifted(): return lax.ppermute(values, 'seq', pairs)  36.2 us
    dot_general x6, matrix products, dot_nt(): lax.dot_general(left, right, (((1,), (1,)), ((), ())), preferred_element_...  30.3 us
    unnamed x150, local copies, waits for them, and re-layouts  30.3 us
    pallas_call x2, Pallas kernels, feed_forward(): pl.pallas_call(feed_forward_kernel, grid=(steps,), in_specs=[whole, in_bl...  29.5 us
  transfers between devices with their start and end apart: 14, of which 1 were waited for; matrix products, arithmetic and copies ran while one was open for 14% of the time, Pallas kernels for 49%

profile of v2, /device:TPU:0, one launch (start us, length us, event | category | flops | bytes accessed | tf_op | source)
XLA Modules:
  0.0 809.8 jit_solution(12856980261036215964)
XLA Ops:
  16.7 120.6 %gather.18 = (bf16[2,2,4,2,32,128]{5,4,3,2,1,0:T(8,128)(2,1)S(1)}, bf16[2,2,4,2,32,4096]{5,4,3,2,1,0:T(8,128)(2,1)}, bf16[2,2,4,2,32,4096]{5,4,3,2,1,0:T(8,128)(...) custom-call(bf16[32,128]{1,0:T(8,128)(2,1)S(1)} %fusion.34.refs_0_, ...), custom_call_target="tpu_custom_call" | custom-call | tf_op jit(solution)/shard_map/gather/pallas_call | solution.py:552
  149.3 15.2 %feed_forward.2 = (bf16[512,4096]{1,0:T(8,128)(2,1)}, bf16[512,4096]{1,0:T(8,128)(2,1)}, f32[512,1024]{1,0:T(8,128)S(1)}) custom-call(bf16[512,1024]{1,0:T(8,128)(2,1)S(1)} %multiply_convert_fusion.10.hid_ref.refs_12_, bf16[1024,4096]{1,0:T(8,128)(2,1)} %bitcast.144, bf16[1024,4096]{1,0:T(8,128)(2,1)} %bitcast.146), custom_call_target="tpu_custom_call" | custom-call | flops 8589934592 | bytes 25165824 | tf_op jit(solution)/shard_map/feed_forward/pallas_call | solution.py:1064
  166.1 7.4 collective-permute-start
  182.3 15.8 %fusion = (bf16[2048,512]{1,0:T(8,128)(2,1)S(1)}, bf16[2048,512]{1,0:T(8,128)(2,1)S(1)}) fusion(f32[512]{0:T(512)S(1)} %negate_power_fusion, f32[2048]{0:T(1024)S(1)} %subtract_convert_fusion), kind=kLoop, calls=%fused_computation.3 | loop fusion | flops 3145728 | bytes 4204544 | tf_op jit(solution)/shard_map/convert.20
  202.9 50.2 %positions.1.pos_ref = f32[16,512,1536]{2,1,0:T(8,128)} custom-call(bf16[512,1024]{1,0:T(8,128)(2,1)S(1)} %convolution_convert_fusion.3.q_ref, bf16[2048,1024]{1,0:T(8,128)(2,1)S(1)} %convolution_convert_fusion.2.r_ref, bf16[1,1024]{1,0:T(2,128)(2,1)S(1)} %get-tuple-element.254.b_ref), custom_call_target="tpu_custom_call" | custom-call | flops 17179869184 | bytes 55576576 | tf_op jit(solution)/shard_map/positions/pallas_call | solution.py:163
  267.7 4.8 convolution_convert_fusion.v_ref
  272.5 4.8 convolution_convert_fusion.1.k_ref
  277.3 53.8 %attend.1 = (bf16[512,1024]{1,0:T(8,128)(2,1)S(1)}, bf16[16,512,1536]{2,1,0:T(8,128)(2,1)}, f32[512,1024]{1,0:T(8,128)S(1)}) custom-call(s32[1]{0:T(128)} %select_n.93.live_ref, bf16[512,1024]{1,0:T(8,128)(2,1)S(1)} %copy-done.18, bf16[1536,1024]{1,0:T(8,128)(2,1)} %convolution_convert_fusion.1.k_ref, bf16[1536,1024]{1,0:T(8,128)(2,1)} %convolution_convert_fusion.v_ref, ...), custom_call_target="tpu_custom_call" | custom-call | flops 25769803776 | bytes 85985280 | tf_op jit(solution)/shard_map/attend/pallas_call | solution.py:163
  339.0 5.3 fusion.4
  351.5 6.2 fusion.42
  359.5 7.6 depthwise.1
  375.0 14.4 %feed_forward.3 = (bf16[512,4096]{1,0:T(8,128)(2,1)}, bf16[512,4096]{1,0:T(8,128)(2,1)}, f32[512,1024]{1,0:T(8,128)S(1)}) custom-call(bf16[512,1024]{1,0:T(8,128)(2,1)S(1)} %multiply_convert_fusion.5.hid_ref.refs_0_, bf16[1024,4096]{1,0:T(8,128)(2,1)} %get-tuple-element.227.in_ref, bf16[1024,4096]{1,0:T(8,128)(2,1)} %get-tuple-element.226.out_w_ref), custom_call_target="tpu_custom_call" | custom-call | flops 8589934592 | bytes 25165824 | tf_op jit(solution)/shard_map/feed_forward/pallas_call | solution.py:1064
  394.3 14.2 %feed_forward_back.2 = (bf16[512,4096]{1,0:T(8,128)(2,1)}, f32[512,1024]{1,0:T(8,128)S(1)}) custom-call(bf16[512,1024]{1,0:T(8,128)(2,1)S(1)} %get-tuple-element.218.low_ref.refs_3_, bf16[1024,4096]{1,0:T(8,128)(2,1)} %get-tuple-element.227.in_ref, bf16[1024,4096]{1,0:T(8,128)(2,1)} %get-tuple-element.226.out_w_ref, ...), custom_call_target="tpu_custom_call" | custom-call | flops 8589934592 | bytes 25165824 | tf_op jit(solution)/shard_map/feed_forward_back/pallas_call | solution.py:1085
  411.5 18.4 %products.1 = bf16[1024,9216]{1,0:T(8,128)(2,1)} custom-call(bf16[512,1024]{1,0:T(8,128)(2,1)S(1)} %multiply_convert_fusion.5.hid_ref.refs_0_, bf16[512,4096]{1,0:T(8,128)(2,1)} %get-tuple-element.70.refs_1_, bf16[512,4096]{1,0:T(8,128)(2,1)} %get-tuple-element.71.refs_2_, bf16[512,1024]{1,0:T(8,128)(2,1)S(1)} %get-tuple-element.218.low_ref.refs_3_, ...), custom_call_target="tpu_custom_call" | custom-call | flops 9663676416 | bytes 33030144 | tf_op jit(solution)/shard_map/products/pallas_call | solution.py:917
  449.3 11.2 %depthwise_back.1 = (f32[512,1024]{1,0:T(8,128)}, f32[31,1024]{1,0:T(8,128)}) custom-call(f32[542,1024]{1,0:T(8,128)} %pad_maximum_fusion.1.wide_ref, f32[542,1024]{1,0:T(8,128)} %pad_maximum_fusion.2.grad_ref, f32[31,1024]{1,0:T(8,128)} %slice.210.taps_ref), custom_call_target="tpu_custom_call" | custom-call | flops 68820992 | bytes 6660096 | tf_op jit(solution)/shard_map/depthwise_back/pallas_call | solution.py:1151
  464.8 5.6 multiply_reduce_fusion.3
  475.6 30.9 %keys_back.1 = (bf16[16,512,1536]{2,1,0:T(8,128)(2,1)}, bf16[1536,1024]{1,0:T(8,128)(2,1)}, bf16[1536,1024]{1,0:T(8,128)(2,1)}) custom-call(bf16[512,1024]{1,0:T(8,128)(2,1)} %copy-done.17, bf16[1536,1024]{1,0:T(8,128)(2,1)} %convolution_convert_fusion.v_ref, bf16[1,1024]{1,0:T(2,128)(2,1)} %copy-done.11, bf16[512,1024]{1,0:T(8,128)(2,1)} %fusion.26.g_ref, ...), custom_call_target="tpu_custom_call" | custom-call | flops 38654705664 | bytes 65013760 | tf_op jit(solution)/shard_map/keys_back/pallas_call | solution.py:262
  506.4 5.5 fusion.51
  514.6 5.7 convert_dynamic-update-slice_fusion
  525.7 5.7 collective-permute-start.11
  534.0 56.5 %queries_back.1 = (bf16[512,1024]{1,0:T(8,128)(2,1)}, bf16[2048,1024]{1,0:T(8,128)(2,1)}, f32[1,1024]{1,0:T(1,128)}, f32[1,1024]{1,0:T(1,128)}) custom-call(bf16[512,1024]{1,0:T(8,128)(2,1)} %copy-done.17, bf16[1536,1024]{1,0:T(8,128)(2,1)} %convolution_convert_fusion.1.k_ref, bf16[2048,1024]{1,0:T(8,128)(2,1)} %copy-done.19, bf16[1,1024]{1,0:T(2,128)(2,1)} %copy-done.10, ...), custom_call_target="tpu_custom_call" | custom-call | flops 47244640256 | bytes 38807552 | tf_op jit(solution)/shard_map/queries_back/pallas_call | solution.py:262
  594.9 5.3 multiply_reduce_fusion.4
  602.4 14.6 %feed_forward_back.3 = (bf16[512,4096]{1,0:T(8,128)(2,1)}, f32[512,1024]{1,0:T(8,128)S(1)}) custom-call(bf16[512,1024]{1,0:T(8,128)(2,1)S(1)} %get-tuple-element.210.low_ref.refs_15_, bf16[1024,4096]{1,0:T(8,128)(2,1)} %bitcast.145, bf16[1024,4096]{1,0:T(8,128)(2,1)} %bitcast.147, bf16[512,4096]{1,0:T(8,128)(2,1)} %get-tuple-element.82.slope_ref), custom_call_target="tpu_custom_call" | custom-call | flops 8589934592 | bytes 25165824 | tf_op jit(solution)/shard_map/feed_forward_back/pallas_call | solution.py:1085
  623.3 164.6 %scatter.1 = (f32[32,128]{1,0:T(8,128)}, f32[7,32,1024]{2,1,0:T(8,128)}, f32[32,4096]{1,0:T(8,128)}, f32[128,1024]{1,0:T(8,128)}) custom-call(bf16[2,2,4,2,32,128]{5,4,3,2,1,0:T(8,128)(2,1)} %bitcast.119, bf16[512,1024]{1,0:T(8,128)(2,1)} %copy-done.4, bf16[512,1024]{1,0:T(8,128)(2,1)} %copy-done.42, bf16[512,1024]{1,0:T(8,128)(2,1)} %copy-done.41, ...), custom_call_target="tpu_custom_call" | custom-call | tf_op jit(solution)/shard_map/scatter/pallas_call | solution.py:855
  (295 shorter events, 146.6 us)
Async XLA Ops:
  7.2 249.7 %copy-start = (s32[1,8]{1,0:T(1,128)S(1)}, s32[1,8]{1,0:T(1,128)}, u32[]{:S(2)}) copy-start(s32[1,8]{1,0:T(1,128)} %param.26) | copy-start | bytes 100
  7.2 135.2 %copy-start.48 = (bf16[128,1024]{1,0:T(8,128)(2,1)S(1)}, bf16[128,1024]{1,0:T(8,128)(2,1)}, u32[]{:S(2)}) copy-start(bf16[128,1024]{1,0:T(8,128)(2,1)} %param.45) | copy-start | bytes 786436
  7.2 135.5 %copy-start.55 = (bf16[32,1024]{1,0:T(8,128)(2,1)S(1)}, bf16[32,1024]{1,0:T(8,128)(2,1)}, u32[]{:S(2)}) copy-start(bf16[32,1024]{1,0:T(8,128)(2,1)} %param.37) | copy-start | bytes 196612
  7.2 135.5 %copy-start.50 = (bf16[32,2048]{1,0:T(8,128)(2,1)S(1)}, bf16[32,2048]{1,0:T(8,128)(2,1)}, u32[]{:S(2)}) copy-start(bf16[32,2048]{1,0:T(8,128)(2,1)} %param.39) | copy-start | bytes 393220
  7.2 325.1 %all-gather.2.cloned.1.call-start = ((), (), s32[]{:S(2)}) async-start(), calls=%async_computation.1 | async-start | bytes 25952256 | tf_op jit(solution)/shard_map/all_gather | solution.py:1174
  8.2 134.6 %copy-start.56 = (bf16[32,1024]{1,0:T(8,128)(2,1)S(1)}, bf16[32,1024]{1,0:T(8,128)(2,1)}, u32[]{:S(2)}) copy-start(bf16[32,1024]{1,0:T(8,128)(2,1)} %param.42) | copy-start | bytes 196612
  144.7 649.3 %reduce-scatter.2.cloned.1.call-start = ((), (), s32[]{:S(2)}) async-start(), calls=%async_computation.2 | async-start | bytes 19464192 | tf_op jit(solution)/shard_map/reduce_scatter | solution.py:1185
  148.9 113.4 %copy-start.51 = (f32[1,1024]{1,0:T(1,128)}, f32[1,1024]{1,0:T(1,128)S(1)}, u32[]{:S(2)}) copy-start(f32[1,1024]{1,0:T(1,128)S(1)} %get-tuple-element.252) | copy-start | bytes 12292
  164.8 97.6 %copy-start.59 = (f32[512]{0:T(512)}, f32[512]{0:T(512)S(1)}, u32[]{:S(2)}) copy-start(f32[512]{0:T(512)S(1)} %broadcast_multiply_fusion.16) | copy-start | bytes 6148
  165.2 97.2 %copy-start.63 = (f32[512]{0:T(512)}, f32[512]{0:T(512)S(1)}, u32[]{:S(2)}) copy-start(f32[512]{0:T(512)S(1)} %add_rsqrt_fusion.4) | copy-start | bytes 6148
  166.1 93.4 %collective-permute-start = (bf16[512,1024]{1,0:T(8,128)(2,1)S(1)}, bf16[512,1024]{1,0:T(8,128)(2,1)}, u32[]{:S(2)}, u32[]{:S(2)}) collective-permute-start(bf16[512,1024]{1,0:T(8,128)(2,1)S(1)} %multiply_convert_fusion.9.refs_5_), channel_id=1, source_target_pairs={{0,2},{1,3},{2,4},{3,5},{4,6},{5,7},{8,10},{9,11},{10,12},{11,13},... | collective-permute-start | bytes 3145736 | tf_op jit(solution)/shard_map/ppermute | solution.py:1170
  173.5 87.5 %collective-permute-start.1 = (bf16[512,1024]{1,0:T(8,128)(2,1)S(1)}, bf16[512,1024]{1,0:T(8,128)(2,1)}, u32[]{:S(2)}, u32[]{:S(2)}) collective-permute-start(bf16[512,1024]{1,0:T(8,128)(2,1)S(1)} %multiply_convert_fusion.9.refs_5_), channel_id=1, source_target_pairs={{0,1},{1,2},{2,3},{3,4},{4,5},{5,6},{6,7},{8,9},{9,10},{10,11},{11... | collective-permute-start | bytes 3145736 | tf_op jit(solution)/shard_map/ppermute | solution.py:1170
  176.6 86.1 %collective-permute-start.2 = (bf16[512,1024]{1,0:T(8,128)(2,1)S(1)}, bf16[512,1024]{1,0:T(8,128)(2,1)}, u32[]{:S(2)}, u32[]{:S(2)}) collective-permute-start(bf16[512,1024]{1,0:T(8,128)(2,1)S(1)} %multiply_convert_fusion.9.refs_5_), channel_id=1, source_target_pairs={{1,0},{2,1},{3,2},{4,3},{5,4},{6,5},{7,6},{9,8},{10,9},{11,10},{12... | collective-permute-start | bytes 3145736 | tf_op jit(solution)/shard_map/ppermute | solution.py:1170
  177.9 86.1 %collective-permute-start.3 = (bf16[512,1024]{1,0:T(8,128)(2,1)S(1)}, bf16[512,1024]{1,0:T(8,128)(2,1)}, u32[]{:S(2)}, u32[]{:S(2)}) collective-permute-start(bf16[512,1024]{1,0:T(8,128)(2,1)S(1)} %multiply_convert_fusion.9.refs_5_), channel_id=1, source_target_pairs={{2,0},{3,1},{4,2},{5,3},{6,4},{7,5},{10,8},{11,9},{12,10},{13,11},... | collective-permute-start | bytes 3145736 | tf_op jit(solution)/shard_map/ppermute | solution.py:1170
  180.9 96.4 %copy-start.11 = (bf16[1,1024]{1,0:T(2,128)(2,1)}, bf16[1,1024]{1,0:T(2,128)(2,1)S(1)}, u32[]{:S(2)}) copy-start(bf16[1,1024]{1,0:T(2,128)(2,1)S(1)} %get-tuple-element.255.u_ref) | copy-start | bytes 6148
  346.4 11.3 %collective-permute-start.4 = (bf16[15,1024]{1,0:T(8,128)(2,1)S(1)}, bf16[15,1024]{1,0:T(8,128)(2,1)S(1)}, u32[]{:S(2)}, u32[]{:S(2)}) collective-permute-start(bf16[15,1024]{1,0:T(8,128)(2,1)S(1)} %get-tuple-element.237), channel_id=1, source_target_pairs={{0,1},{1,2},{2,3},{3,4},{4,5},{5,6},{6,7},{8,9},{9,10},{10,11},{11... | collective-permute-start | bytes 92168 | tf_op jit(solution)/shard_map/ppermute | solution.py:1170
  350.2 7.6 collective-permute-start.5
  435.8 8.3 %collective-permute-start.6 = (bf16[15,1024]{1,0:T(8,128)(2,1)S(1)}, bf16[15,1024]{1,0:T(8,128)(2,1)S(1)}, u32[]{:S(2)}, u32[]{:S(2)}) collective-permute-start(bf16[15,1024]{1,0:T(8,128)(2,1)S(1)} %get-tuple-element.235), channel_id=1, source_target_pairs={{0,1},{1,2},{2,3},{3,4},{4,5},{5,6},{6,7},{8,9},{9,10},{10,11},{11... | collective-permute-start | bytes 92168 | tf_op jit(solution)/shard_map/ppermute | solution.py:1170
  442.8 4.8 collective-permute-start.7
  521.7 71.8 %collective-permute-start.10 = (bf16[512,1024]{1,0:T(8,128)(2,1)}, bf16[512,1024]{1,0:T(8,128)(2,1)}, u32[]{:S(2)}, u32[]{:S(2)}) collective-permute-start(bf16[512,1024]{1,0:T(8,128)(2,1)} %get-tuple-element.232), channel_id=1, source_target_pairs={{0,1},{1,2},{2,3},{3,4},{4,5},{5,6},{6,7},{8,9},{9,10},{10,11},{11... | collective-permute-start | bytes 3145736 | tf_op jit(solution)/shard_map/ppermute | solution.py:1170
  525.7 67.8 %collective-permute-start.11 = (bf16[512,1024]{1,0:T(8,128)(2,1)S(1)}, bf16[512,1024]{1,0:T(8,128)(2,1)}, u32[]{:S(2)}, u32[]{:S(2)}) collective-permute-start(bf16[512,1024]{1,0:T(8,128)(2,1)S(1)} %get-tuple-element.231), channel_id=1, source_target_pairs={{0,2},{1,3},{2,4},{3,5},{4,6},{5,7},{8,10},{9,11},{10,12},{11,13},... | collective-permute-start | bytes 3145736 | tf_op jit(solution)/shard_map/ppermute | solution.py:1170
  531.4 62.1 %collective-permute-start.8 = (bf16[512,1024]{1,0:T(8,128)(2,1)S(1)}, bf16[512,1024]{1,0:T(8,128)(2,1)}, u32[]{:S(2)}, u32[]{:S(2)}) collective-permute-start(bf16[512,1024]{1,0:T(8,128)(2,1)S(1)} %get-tuple-element.230), channel_id=1, source_target_pairs={{2,0},{3,1},{4,2},{5,3},{6,4},{7,5},{10,8},{11,9},{12,10},{13,11},... | collective-permute-start | bytes 3145736 | tf_op jit(solution)/shard_map/ppermute | solution.py:1170
  532.7 60.8 %collective-permute-start.9 = (bf16[512,1024]{1,0:T(8,128)(2,1)S(1)}, bf16[512,1024]{1,0:T(8,128)(2,1)}, u32[]{:S(2)}, u32[]{:S(2)}) collective-permute-start(bf16[512,1024]{1,0:T(8,128)(2,1)S(1)} %get-tuple-element.233), channel_id=1, source_target_pairs={{1,0},{2,1},{3,2},{4,3},{5,4},{6,5},{7,6},{9,8},{10,9},{11,10},{12... | collective-permute-start | bytes 3145736 | tf_op jit(solution)/shard_map/ppermute | solution.py:1170
  534.0 59.5 %copy-start.52 = (f32[1,1024]{1,0:T(1,128)S(1)}, f32[1,1024]{1,0:T(1,128)}, u32[]{:S(2)}) copy-start(f32[1,1024]{1,0:T(1,128)} %copy-done.51) | copy-start | bytes 12292
  (59 other events, 560.7 us)
Sparse Core Ops, SparseCore 0:
  144.8 186.1 all-gather.1
  430.0 232.8 reduce-scatter.1
